TPU v7x, 32 devices: a whole 2x2x4 slice. The times are simulated.
32 devices in a mesh: det: 4 (over x, core), tm: 8 (over z, y).
Axes of the slice: x: 2, y: 2, z: 4, core: 2. Of those that a mesh axis runs over, the one named last changes fastest.
Arguments:
- sky_map: bfloat16 [32, 3, 128, 128], P('tm', None, 'det'), may hold values from -6 to 6
- tile_home: int32 [32], replicated, may hold values from 0 to 31, as said below
- piece_tiles: int32 [4, 8, 32], P('det', 'tm'), may hold values from 0 to 31, as said below
- run_slot: int32 [32, 128], P('det', 'tm'), may hold values from 0 to 31
- hit_row: int32 [32, 16384], P('det', 'tm'), may hold values from 0 to 126
- hit_col: int32 [32, 16384], P('det', 'tm'), may hold values from 0 to 126
- frac_row: bfloat16 [32, 16384], P('det', 'tm'), may hold values from 0 to 1
- frac_col: bfloat16 [32, 16384], P('det', 'tm'), may hold values from 0 to 1
- angle: float32 [32, 16384], P('det', 'tm'), may hold values from -3.140625 to 3.140625
- noise_coef: float32 [32, 1025], P('det'), may hold values from -0.3 to 0.3
Outputs:
- normal_map: float32 [32, 3, 128, 128], P('tm', None, 'det')
Inputs may be any that keep to these rules, and one draw needn't show every extreme that they name: A permutation: tile g lies in row tile_home[g] of sky_map. `piece_tiles`: the 32 tiles listed by one piece are distinct, and at most 4 of them lie in rows of one index of tm (rows o * 4 to o * 4 + 3 of sky_map); every piece has exactly 4 tile in each index of tm that it reads from.
All inputs are finite; a program needn't handle non-finite values.
Results may differ from a plain program's by a relative error of at most 0.0048.
Values may be sent and summed in bfloat16 or wider, within the bound.
No kernel may reach another device: no remote copies, remote signals or barrier semaphores. Data moves between devices by JAX's collectives and lax.ppermute only.
A program may use at most 128 MiB of HBM per device.

v0:
```python
import functools
import math

import jax
import jax.numpy as jnp
from jax import lax
from jax.experimental import pallas as pl
from jax.experimental.pallas import tpu as pltpu
from jax.sharding import PartitionSpec as P

LISTED = 32


block_cols = 128
group_runs = 32


def extended_2(cells, sides, width):
    for axis, dim in sides:
        count = lax.axis_size(axis)
        ends = count - 1
        head = lax.slice_in_dim(cells, 0, width, axis=dim)
        tail = lax.slice_in_dim(cells, cells.shape[dim] - width, cells.shape[dim], axis=dim)
        cells = jnp.concatenate(
            [
                lax.ppermute(tail, axis, [(i, (i + 1) % count) for i in range(ends)]),
                cells,
                lax.ppermute(head, axis, [((i + 1) % count, i) for i in range(ends)]),
            ],
            axis=dim,
        )
    return cells


def positions_of(piece_list, tile_home):
    table_rows = jnp.arange(tile_home.shape[0], dtype=jnp.int32)
    matched = piece_list[:, None] == table_rows[None, :]
    return jnp.sum(jnp.where(matched, tile_home[None, :], 0), axis=1)


def run_weights(pixel_index, upper_frac, side_len):
    lower_weight = (1.0 - upper_frac.astype(jnp.float32)).astype(jnp.bfloat16)
    pixels = lax.broadcasted_iota(jnp.int32, pixel_index.shape + (side_len,), pixel_index.ndim)
    zero_value = jnp.zeros((), jnp.bfloat16)
    low_part = jnp.where(pixels == pixel_index[..., None], lower_weight[..., None], zero_value)
    high_part = jnp.where(pixels == pixel_index[..., None] + 1, upper_frac[..., None], zero_value)
    return low_part + high_part


def responses(angles):
    twice = 2.0 * angles
    return jnp.stack([jnp.ones_like(twice), jnp.cos(twice), jnp.sin(twice)], axis=1)


def banded(signal, noise_coef):
    det_count = signal.shape[0]
    half_band = noise_coef.shape[1] - 1
    reach_blocks = half_band // block_cols
    span_cols = (2 * reach_blocks + 1) * block_cols
    weights = jnp.concatenate([noise_coef[:, :1] + 1.0, noise_coef[:, 1:]], axis=1)
    zero_pad = jnp.zeros((det_count, block_cols - 1), jnp.float32)
    kernel_row = jnp.concatenate(
        [
            zero_pad,
            weights[:, ::-1],
            weights[:, 1:],
            zero_pad,
            jnp.zeros((det_count, 1), jnp.float32),
        ],
        axis=1,
    )
    period = span_cols + block_cols
    tiled_rows = jnp.tile(kernel_row, (1, block_cols))[:, : block_cols * (period - 1)]
    tiled_rows = tiled_rows.reshape(det_count, block_cols, period - 1)
    matrix = tiled_rows[:, :, block_cols - 1 : block_cols - 1 + span_cols]
    matrix = matrix.reshape(det_count, block_cols, 2 * reach_blocks + 1, block_cols)
    extended = extended_2(signal, (("tm", 1),), half_band)
    block_count = signal.shape[1] // block_cols
    blocks = extended.reshape(det_count, block_count + 2 * reach_blocks, block_cols)
    stacked = jnp.stack(
        [blocks[:, offset : offset + block_count] for offset in range(2 * reach_blocks + 1)], axis=1
    )
    result = jnp.einsum(
        "diml,dmnl->dni",
        matrix,
        stacked,
        precision=lax.Precision.HIGHEST,
        preferred_element_type=jnp.float32,
    )
    return result.reshape(det_count, block_count * block_cols)


GROUP = 4
META = 16
VMEM_LIMIT = 48 * 1024 * 1024
f32 = jnp.float32
bf16 = jnp.bfloat16


def round_up(value, step):
    return -(-value // step) * step


def iota(shape, dim):
    return lax.broadcasted_iota(jnp.int32, shape, dim)


def dot_nn(a, b):
    return lax.dot_general(a, b, (((1,), (0,)), ((), ())), preferred_element_type=f32)


def dot_nt(a, b):
    return lax.dot_general(a, b, (((1,), (1,)), ((), ())), preferred_element_type=f32)


def ones_where(mask):
    return jnp.where(mask, 1.0, 0.0).astype(bf16)


def pack_kernel(owners, cap, tile_dev, pt_ref, th_ref, slot_ref, r_ref, c_ref, fr_ref, fc_ref, ang_ref, out_ref, meta_ref):
    dets, blocks = slot_ref.shape
    runs = dets * blocks
    width = r_ref.shape[1] // blocks
    listed = pt_ref.shape[0]
    spread = dot_nn(
        slot_ref[...].astype(f32).astype(bf16),
        ones_where(iota((blocks, runs), 1) // dets == iota((blocks, runs), 0)),
    )
    run_id = iota((dets, runs), 1)
    own_det = run_id % dets == iota((dets, runs), 0)
    slot_row = jnp.sum(jnp.where(own_det, spread, 0.0), axis=0, keepdims=True)
    slot_row = slot_row.astype(jnp.int32)
    owner_row = jnp.zeros((1, runs), jnp.int32)
    tile_row = jnp.zeros((1, runs), jnp.int32)
    for k in range(listed):
        pos = th_ref[pt_ref[k]]
        own = lax.div(pos, jnp.int32(tile_dev))
        owner_row = jnp.where(slot_row == k, own, owner_row)
        tile_row = jnp.where(slot_row == k, pos - own * tile_dev, tile_row)
    owner_hot = iota((owners, runs), 0) == owner_row
    owner_one = ones_where(owner_hot)
    before = ones_where(iota((runs, runs), 0) < iota((runs, runs), 1))
    prefix = dot_nn(owner_one, before)
    rank = jnp.sum(jnp.where(owner_hot, prefix, 0.0), axis=0, keepdims=True).astype(jnp.int32)
    counts = dot_nt(jnp.ones((8, runs), bf16), owner_one)
    dest = jnp.where(rank < cap, owner_row * cap + rank, -1)
    place = ones_where(iota((owners * cap, runs), 0) == dest)

    def by_run(ref):
        return jnp.concatenate(
            [ref[:, b * width : (b + 1) * width].astype(f32) for b in range(blocks)], axis=0
        )

    angle = by_run(ang_ref)
    angle_high = angle.astype(bf16)
    angle_low = (angle - angle_high.astype(f32)).astype(bf16)
    fields = [by_run(ref).astype(bf16) for ref in (r_ref, c_ref, fr_ref, fc_ref)]
    fields += [angle_high, angle_low]
    for f, field in enumerate(fields):
        sent = dot_nn(place, field).astype(bf16)
        for o in range(owners):
            out_ref[o, f * cap : (f + 1) * cap, :] = sent[o * cap : (o + 1) * cap]
    sub = iota((8, runs), 0)
    lane_run = iota((8, runs), 1)
    facts = jnp.where(sub == 0, tile_row + 1, jnp.where(sub == 1, lane_run // dets, lane_run % dets))
    facts = dot_nt(facts.astype(f32).astype(bf16), place)
    meta_ref[...] = jnp.zeros_like(meta_ref)
    for o in range(owners):
        meta_ref[o, 0:8, 0:cap] = facts[:, o * cap : (o + 1) * cap]
        meta_ref[o, 8:16, 0:owners] = counts
    out_ref[:, len(fields) * cap :, :] = meta_ref[...].astype(bf16)


def weights_of(index, high, shape):
    rows = iota(shape, 0)
    low = (1.0 - high).astype(bf16).astype(f32)
    return jnp.where(rows == index, low, jnp.where(rows == index + 1, high, 0.0))


def project_kernel(
    cap, kept, recv_ref, tiles_ref, out_ref, fields_ref, ids_ref, seg_ref, scratch_ref, sig_ref, lanes_ref
):
    owners = recv_ref.shape[0]
    slots = owners * cap
    width = recv_ref.shape[2]
    groups_det, tile_dev, rows_dev, side = tiles_ref.shape
    part = rows_dev // 3
    for s in range(owners):
        lanes_ref[:, s * cap : (s + 1) * cap] = recv_ref[s, 6 * cap : 6 * cap + META, :].astype(f32)[0:8, 0:cap]
    facts = lanes_ref[...]
    tile1 = facts[0:1].astype(jnp.int32)
    tile_hot = iota((8, slots), 0) + 1 == tile1
    tile_one = ones_where(tile_hot)
    before = ones_where(iota((slots, slots), 0) < iota((slots, slots), 1))
    prefix = dot_nn(tile_one, before)
    count = jnp.sum(jnp.where(tile_hot, 1.0, 0.0), axis=1, keepdims=True)
    padded = jnp.floor((count + (GROUP - 1)) * (1.0 / GROUP)) * GROUP
    padded = jnp.broadcast_to(padded, (8, width))
    start = jnp.zeros((8, width), f32)
    for tile in range(tile_dev - 1):
        start += jnp.where(iota((8, width), 0) > tile, padded[tile : tile + 1], 0.0)
    stop = jnp.minimum(start + padded, float(kept))
    seg_ref[0:8, :] = start
    seg_ref[8:16, :] = stop
    at = 6 * cap + 8
    counts = jnp.concatenate([recv_ref[s, at : at + 8, :].astype(f32)[0:1] for s in range(owners)], axis=0)
    most = jnp.max(jnp.max(counts, axis=0, keepdims=True), axis=1, keepdims=True)
    fullest = jnp.max(jnp.sum(counts, axis=0, keepdims=True), axis=1, keepdims=True)
    over = jnp.logical_or(most > cap, fullest + tile_dev * (GROUP - 1) > kept)
    seg_ref[16:24, :] = jnp.broadcast_to(jnp.where(over, 1.0, 0.0), (8, width))
    where_to = jnp.sum(jnp.where(tile_hot, prefix + start[:, 0:1], 0.0), axis=0, keepdims=True)
    where_to = jnp.where(tile1 > 0, where_to, -1.0).astype(jnp.int32)
    order = ones_where(iota((kept, slots), 0) == where_to)
    source = (iota((1, slots), 1) // cap).astype(f32)
    sub = iota((8, slots), 0)
    facts = jnp.where(sub == 0, jnp.where(tile1 > 0, 1.0, 0.0), jnp.where(sub == 3, source, facts))
    facts = facts.astype(bf16)
    id_lanes = dot_nt(facts, order)
    scratch_ref[...] = jnp.zeros_like(scratch_ref)
    for q in range(-(-kept // width)):
        many = min(width, kept - q * width)
        scratch_ref[q * 8 : q * 8 + 8, 0:many] = id_lanes[:, q * width : q * width + many]
    ids_ref[...] = dot_nt(order, facts)
    sorted_fields = []
    for f in range(6):
        field = jnp.concatenate([recv_ref[s, f * cap : (f + 1) * cap, :] for s in range(owners)], axis=0)
        sorted_fields.append(dot_nn(order, field))
    twice = 2.0 * (sorted_fields[4] + sorted_fields[5])
    for f in range(4):
        fields_ref[f] = sorted_fields[f]
    fields_ref[4] = jnp.cos(twice)
    fields_ref[5] = jnp.sin(twice)
    sig_ref[...] = jnp.zeros_like(sig_ref)
    for tile in range(tile_dev):
        rows = jnp.concatenate([tiles_ref[d, tile] for d in range(groups_det)], axis=0)
        first = jnp.max(start[tile : tile + 1, :]).astype(jnp.int32) // GROUP
        last = jnp.max(stop[tile : tile + 1, :]).astype(jnp.int32) // GROUP

        def step(g, carry, rows=rows):
            base = g * GROUP
            cols = []
            for k in range(GROUP):
                c = fields_ref[1, pl.ds(base + k, 1), :].astype(jnp.int32)
                fc = fields_ref[3, pl.ds(base + k, 1), :]
                cols.append(weights_of(c, fc, (side, width)).astype(bf16))
            partial_rows = dot_nn(rows, jnp.concatenate(cols, axis=1))
            for k in range(GROUP):
                r = fields_ref[0, pl.ds(base + k, 1), :].astype(jnp.int32)
                fr = fields_ref[2, pl.ds(base + k, 1), :]
                row_weight = weights_of(r, fr, (side, width))
                values = []
                for p in range(3):
                    total = None
                    for d in range(groups_det):
                        at = d * rows_dev + p * part
                        term = partial_rows[at : at + part, k * width : (k + 1) * width]
                        term = term * row_weight[d * part : (d + 1) * part]
                        total = term if total is None else total + term
                    values.append(jnp.sum(total, axis=0, keepdims=True))
                cos = fields_ref[4, pl.ds(base + k, 1), :]
                sin = fields_ref[5, pl.ds(base + k, 1), :]
                sig_ref[pl.ds(base + k, 1), :] = values[0] + cos * values[1] + sin * values[2]
            return carry

        lax.fori_loop(first, last, step, 0)
    sent = sig_ref[...].astype(bf16)
    notes = scratch_ref[...].astype(bf16)

    def copy(o, carry):
        out_ref[o, 0:kept, :] = sent
        out_ref[o, kept:, :] = notes
        return carry

    lax.fori_loop(0, owners, copy, 0)


def toeplitz_kernel(line_ref, out_ref):
    width = out_ref.shape[2] // 2
    blocks = out_ref.shape[1] // width
    for m in range(blocks):
        at = (blocks - 1 - m) * width
        piece = jnp.broadcast_to(line_ref[0, :, at : at + 2 * width], (width, 2 * width))
        block = pltpu.roll(piece, width, 1, stride=1, stride_axis=0)[:, :width]
        high = block.astype(bf16)
        out_ref[0, m * width : (m + 1) * width, :width] = high
        out_ref[0, m * width : (m + 1) * width, width:] = (block - high.astype(f32)).astype(bf16)


def filter_kernel(kept, blocks_dev, recv_ref, mat_ref, out_ref, line_ref):
    det = pl.program_id(0)
    owners = recv_ref.shape[0]
    width = recv_ref.shape[2]
    count = owners * blocks_dev
    spans = mat_ref.shape[1] // width
    edge = spans // 2
    line_ref[...] = jnp.zeros_like(line_ref)
    rows = iota((count, kept), 0)

    def one(o, carry):
        notes = recv_ref[o, kept:, :].astype(f32)
        notes = jnp.concatenate([notes[q * 8 : q * 8 + 8] for q in range(notes.shape[0] // 8)], axis=1)[:, :kept]
        at = notes[3:4] * blocks_dev + notes[1:2]
        mine = jnp.logical_and(notes[0:1] > 0.5, notes[2:3] == det.astype(f32))
        at = jnp.where(mine, at, -1.0).astype(jnp.int32)
        line_ref[edge : edge + count, :] += dot_nn(ones_where(rows == at), recv_ref[o, 0:kept, :])
        return carry

    lax.fori_loop(0, owners, one, 0, unroll=owners <= 8)
    spread = jnp.concatenate([line_ref[m : m + count, :].astype(bf16) for m in range(spans)], axis=1)
    both = dot_nn(spread, mat_ref[0])
    out_ref[0] = both[:, :width] + both[:, width:]


def back_kernel(
    blocks_dev, core_ref, fields_ref, ids_ref, seg_ref, filt_ref, mine_ref, theirs_ref, scaled_ref, acc_ref
):
    width = fields_ref.shape[2]
    kept = fields_ref.shape[1]
    pairs, tile_dev, rows_dev, side = mine_ref.shape
    part = rows_dev // 3
    core = core_ref[0]
    poison = jnp.where(seg_ref[16:17, :] > 0.5, jnp.nan, 0.0)
    lines, count, _ = filt_ref.shape
    ids = ids_ref[...]
    at = ids[:, 2:3] * count + ids[:, 3:4] * blocks_dev + ids[:, 1:2]
    at = jnp.where(ids[:, 0:1] > 0.5, at, -1.0).astype(jnp.int32)
    filtered = jnp.zeros((kept, 2 * width), f32)
    for d in range(lines):
        line = filt_ref[d]
        high = line.astype(bf16)
        pair = jnp.concatenate([high, (line - high.astype(f32)).astype(bf16)], axis=1)
        filtered += dot_nn(ones_where(iota((kept, count), 1) + d * count == at), pair)
    filtered = filtered[:, :width] + filtered[:, width:]
    scaled_ref[0] = filtered
    scaled_ref[1] = filtered * fields_ref[4]
    scaled_ref[2] = filtered * fields_ref[5]
    for tile in range(tile_dev):
        first = jnp.max(seg_ref[tile : tile + 1, :]).astype(jnp.int32) // GROUP
        last = jnp.max(seg_ref[8 + tile : 9 + tile, :]).astype(jnp.int32) // GROUP
        acc_ref[...] = jnp.zeros_like(acc_ref)

        def step(g, carry):
            base = g * GROUP
            cols, terms = [], []
            for k in range(GROUP):
                c = fields_ref[1, pl.ds(base + k, 1), :].astype(jnp.int32)
                fc = fields_ref[3, pl.ds(base + k, 1), :]
                cols.append(weights_of(c, fc, (side, width)).astype(bf16))
                r = fields_ref[0, pl.ds(base + k, 1), :].astype(jnp.int32)
                fr = fields_ref[2, pl.ds(base + k, 1), :]
                row_weight = weights_of(r, fr, (side, width))
                terms.append(
                    jnp.concatenate(
                        [(scaled_ref[p, pl.ds(base + k, 1), :] * row_weight).astype(bf16) for p in range(3)],
                        axis=0,
                    )
                )
            acc_ref[...] += dot_nt(jnp.concatenate(terms, axis=1), jnp.concatenate(cols, axis=1))
            return carry

        lax.fori_loop(first, last, step, 0)
        for h in range(pairs):
            for p in range(3):
                base = p * side + h * 2 * part
                mine = acc_ref[pl.ds(pl.multiple_of(base + core * part, part), part), :]
                theirs = acc_ref[pl.ds(pl.multiple_of(base + (1 - core) * part, part), part), :]
                mine_ref[h, tile, p * part : (p + 1) * part, :] = mine + poison
                theirs_ref[h, tile, p * part : (p + 1) * part, :] = (theirs + poison).astype(bf16)


def call(kernel, out, scratch=(), **more):
    return pl.pallas_call(
        kernel,
        out_shape=out,
        scratch_shapes=list(scratch),
        compiler_params=pltpu.CompilerParams(vmem_limit_bytes=VMEM_LIMIT),
        **more,
    )


def whole_tiles(
    tiles, position, run_slot, hit_row, hit_col, frac_row, frac_col, angle, noise_coef
):
    owner_total = lax.axis_size("tm")
    groups_det, tile_dev, rows_dev, side_len = tiles.shape
    part = rows_dev // 3
    owned_tiles = tiles.reshape(groups_det, tile_dev, 3, part, side_len)
    owned_tiles = owned_tiles.transpose(1, 2, 0, 3, 4).reshape(tile_dev, 3, side_len, side_len)
    listed_total = position.shape[0]
    per_owner = max(1, listed_total // owner_total)
    slot_total = owner_total * per_owner
    owner_of = position // tile_dev
    local_slot = position % tile_dev
    listing = jnp.arange(listed_total, dtype=jnp.int32)
    earlier_same = (owner_of[:, None] == owner_of[None, :]) & (listing[:, None] > listing[None, :])
    rank_within = jnp.sum(earlier_same.astype(jnp.int32), axis=1)
    outbox_row = owner_of * per_owner + rank_within
    slot_rows = jnp.arange(slot_total, dtype=jnp.int32)
    asked_slot = (
        jnp.sum(
            jnp.where(slot_rows[:, None] == outbox_row[None, :], local_slot[None, :] + 1, 0), axis=1
        )
        - 1
    )
    served_slot = lax.all_to_all(asked_slot, "tm", split_axis=0, concat_axis=0, tiled=True)
    every_tile = lax.all_gather(owned_tiles, "tm", axis=0, tiled=True)
    listed = jnp.take(every_tile, position, axis=0)
    det_local, time_local = hit_row.shape
    run_length = time_local // run_slot.shape[1]
    run_total = det_local * run_slot.shape[1]
    per_group = math.gcd(run_total, group_runs)
    group_total = run_total // per_group

    def grouped(values):
        return values.reshape(group_total, per_group, run_length)

    run_items = (
        run_slot.reshape(group_total, per_group),
        grouped(hit_row),
        grouped(hit_col),
        grouped(frac_row),
        grouped(frac_col),
        grouped(angle),
    )

    def project(items):
        slots, rows_at, cols_at, frac_rows, frac_cols, angles = items
        tiles = jnp.take(listed, slots, axis=0)
        row_weight = run_weights(rows_at, frac_rows, side_len).astype(jnp.float32)
        col_weight = run_weights(cols_at, frac_cols, side_len)
        partial_rows = jnp.einsum(
            "bpij,bsj->bpsi", tiles, col_weight, preferred_element_type=jnp.float32
        )
        values = jnp.sum(partial_rows * row_weight[:, None], axis=3)
        return jnp.sum(values * responses(angles), axis=1)

    signal = lax.map(project, run_items).reshape(det_local, time_local)
    filtered = banded(signal, noise_coef)

    def back_project(carry, items):
        slots, rows_at, cols_at, frac_rows, frac_cols, angles, filt_runs = items
        row_weight = run_weights(rows_at, frac_rows, side_len).astype(jnp.float32)
        col_weight = run_weights(cols_at, frac_cols, side_len)
        scaled = responses(angles) * filt_runs[:, None]
        weighted = (scaled[..., None] * row_weight[:, None]).astype(jnp.bfloat16)
        tile_terms = jnp.einsum(
            "bpsi,bsj->bpij", weighted, col_weight, preferred_element_type=jnp.float32
        )
        return (carry.at[slots].add(tile_terms), None)

    initial = jnp.zeros((listed_total, 3, side_len, side_len), jnp.float32)
    contrib, _ = lax.scan(back_project, initial, run_items + (grouped(filtered),))
    outbox = jnp.zeros((slot_total, 3, side_len, side_len), jnp.float32).at[outbox_row].set(contrib)
    arrived = lax.all_to_all(outbox, "tm", split_axis=0, concat_axis=0, tiled=True)
    summed = jnp.stack(
        [
            jnp.sum(jnp.where((served_slot == slot_id)[:, None, None, None], arrived, 0.0), axis=0)
            for slot_id in range(tile_dev)
        ]
    )
    return lax.psum_scatter(summed, "det", scatter_dimension=2, tiled=True)


def body(
    sky_map,
    tile_home,
    piece_tiles,
    run_slot,
    hit_row,
    hit_col,
    frac_row,
    frac_col,
    angle,
    noise_coef,
):
    owners = lax.axis_size("tm")
    groups_det = lax.axis_size("det")
    tile_dev, _, part, side = sky_map.shape
    dets, blocks = run_slot.shape
    runs = dets * blocks
    width = hit_row.shape[1] // blocks
    listed = piece_tiles.shape[2]
    half_band = noise_coef.shape[1] - 1
    cap = round_up(2 * runs // min(owners, listed), META)
    kept = round_up(runs + runs // 2, META)
    slots = owners * cap
    piece_list = piece_tiles.reshape(listed)
    smem = pl.BlockSpec(memory_space=pltpu.SMEM)
    vmem = pl.BlockSpec(memory_space=pltpu.VMEM)

    packed = call(
        functools.partial(pack_kernel, owners, cap, tile_dev),
        jax.ShapeDtypeStruct((owners, 6 * cap + META, width), bf16),
        [pltpu.VMEM((owners, META, width), f32)],
        in_specs=[smem, smem] + [vmem] * 6,
        out_specs=vmem,
    )(piece_list, tile_home, run_slot, hit_row, hit_col, frac_row, frac_col, angle)
    recv = lax.all_to_all(packed, "tm", split_axis=0, concat_axis=0, tiled=True)
    tiles = lax.all_gather(sky_map.reshape(tile_dev, 3 * part, side), "det", axis=0)

    weights = jnp.concatenate([noise_coef[:, :1] + 1.0, noise_coef[:, 1:]], axis=1)
    line = jnp.concatenate(
        [
            jnp.zeros((dets, width), f32),
            weights[:, ::-1],
            weights[:, 1:],
            jnp.zeros((dets, width - 1), f32),
        ],
        axis=1,
    )
    spans = 2 * (half_band // width) + 1
    matrix = call(
        toeplitz_kernel,
        jax.ShapeDtypeStruct((dets, spans * width, 2 * width), bf16),
        grid=(dets,),
        in_specs=[pl.BlockSpec((1, 1, line.shape[1]), lambda d: (d, 0, 0))],
        out_specs=pl.BlockSpec((1, spans * width, 2 * width), lambda d: (d, 0, 0)),
    )(line[:, None, :])

    notes = round_up(kept, width) // width * 8
    sent, fields, ids, seg = call(
        functools.partial(project_kernel, cap, kept),
        (
            jax.ShapeDtypeStruct((owners, kept + notes, width), bf16),
            jax.ShapeDtypeStruct((6, kept, width), f32),
            jax.ShapeDtypeStruct((kept, 8), f32),
            jax.ShapeDtypeStruct((24, width), f32),
        ),
        [pltpu.VMEM((notes, width), f32), pltpu.VMEM((kept, width), f32), pltpu.VMEM((8, slots), f32)],
    )(recv, tiles)
    heard = lax.all_to_all(sent, "tm", split_axis=0, concat_axis=0, tiled=True)

    count = owners * blocks
    filtered = call(
        functools.partial(filter_kernel, kept, blocks),
        jax.ShapeDtypeStruct((dets, count, width), f32),
        [pltpu.VMEM((count + spans - 1, width), f32)],
        grid=(dets,),
        in_specs=[
            pl.BlockSpec((owners, kept + notes, width), lambda d: (0, 0, 0)),
            pl.BlockSpec((1, spans * width, 2 * width), lambda d: (d, 0, 0)),
        ],
        out_specs=pl.BlockSpec((1, count, width), lambda d: (d, 0, 0)),
    )(heard, matrix)
    place = lax.axis_index("det")
    core = lax.rem(place, 2)
    half = lax.div(place, 2)
    pairs = groups_det // 2
    mine, theirs = call(
        functools.partial(back_kernel, blocks),
        (
            jax.ShapeDtypeStruct((pairs, tile_dev, 3 * part, side), f32),
            jax.ShapeDtypeStruct((pairs, tile_dev, 3 * part, side), bf16),
        ),
        [pltpu.VMEM((3, kept, width), f32), pltpu.VMEM((3 * side, side), f32)],
        in_specs=[smem] + [vmem] * 4,
        out_specs=(vmem, vmem),
    )(core[None].astype(jnp.int32), fields, ids, seg, filtered)

    beside = lax.ppermute(theirs, "det", [(i, i ^ 1) for i in range(groups_det)])

    def of_pair(h):
        pick = lambda values: lax.dynamic_index_in_dim(values, h, 0, keepdims=False).astype(f32)
        return pick(mine) + pick(beside)

    total = of_pair(half)
    for step in range(1, pairs):
        ring = [(i, (i + 2 * step) % groups_det) for i in range(groups_det)]
        total = total + lax.ppermute(
            of_pair(lax.rem(half + step, pairs)).astype(bf16), "det", ring
        ).astype(f32)
    total = total.reshape(tile_dev, 3, part, side)

    def travelling(_):
        position = positions_of(piece_list, tile_home)
        return whole_tiles(
            tiles, position, run_slot, hit_row, hit_col, frac_row, frac_col, angle, noise_coef
        )

    fits = jnp.logical_not(jnp.isnan(total[0, 0, 0, 0]))
    return lax.cond(fits, lambda t: t, travelling, total)


def solution(mesh):
    placed = (
        P("tm", None, "det", None),
        P(),
        P("det", "tm", None),
        P("det", "tm"),
        P("det", "tm"),
        P("det", "tm"),
        P("det", "tm"),
        P("det", "tm"),
        P("det", "tm"),
        P("det", None),
    )
    return jax.shard_map(
        body, mesh=mesh, in_specs=placed, out_specs=P("tm", None, "det", None), check_vma=False
    )
```

profile of v0, /device:TPU:0, one launch (start us, length us, event | category | flops | bytes accessed | tf_op | source)
XLA Modules:
  0.0 94.4 jit_solution(3458441997378222381)
XLA Ops:
  6.5 2.3 %shard_map.102 = bf16[8,208,128]{2,1,0:T(8,128)(2,1)} custom-call(s32[32]{0:T(128)} %bitcast.270, s32[32]{0:T(128)} %th_ref.1, s32[8,16]{1,0:T(8,128)} %slot_ref.1, s32[8,2048]{1,0:T(8,128)} %r_ref.1, s32[8,2048]{1,0:T(8,128)} %c_ref.1, bf16[8,2048]{1,0:T(8,128)(2,1)} %fr_ref.1, bf16[8,2048]{1,0:T(8,128)(2,1)} %fc_ref.1, f32[8,2048]{1,0:T(8,128)} %ang_ref.1), custom_call_target="tpu_custom_call" | custom-call | tf_op jit(solution)/shard_map/pallas_call | solution.py:491
  8.9 7.3 %all-to-all-start.2 = ((bf16[8,208,128]{2,1,0:T(8,128)(2,1)}), bf16[8,208,128]{2,1,0:T(8,128)(2,1)S(1)}, u32[]{:S(2)}, u32[]{:S(2)}) async-start(bf16[8,208,128]{2,1,0:T(8,128)(2,1)} %shard_map.102), calls=%async_computation.3 | async-start | bytes 851968 | tf_op jit(solution)/shard_map/all_to_all | solution.py:498
  16.1 6.7 %all_gather.6.tiles_ref = bf16[4,4,96,128]{3,2,1,0:T(8,128)(2,1)S(1)} all-gather(bf16[1,4,96,128]{3,2,1,0:T(8,128)(2,1)} %bitcast.269), channel_id=1, replica_groups=mesh['det'=4,'tm'=8] {'det'}, dimensions={0}, use_global_device_ids=true | all-gather | bytes 491520 | tf_op jit(solution)/shard_map/all_gather | solution.py:499
  22.8 5.7 %all-to-all-done.2.recv_ref = bf16[8,208,128]{2,1,0:T(8,128)(2,1)S(1)} async-done(((bf16[8,208,128]{2,1,0:T(8,128)(2,1)}), bf16[8,208,128]{2,1,0:T(8,128)(2,1)S(1)}, u32[]{:S(2)}, u32[]{:S(2)}) %all-to-all-start.2) | async-done | bytes 426016 | tf_op jit(solution)/shard_map/all_to_all | solution.py:498
  28.5 12.9 %shard_map.103 = (bf16[8,208,128]{2,1,0:T(8,128)(2,1)}, f32[6,192,128]{2,1,0:T(8,128)S(1)}, f32[192,8]{1,0:T(8,128)S(1)}, f32[24,128]{1,0:T(8,128)S(1)}) custom-call(bf16[8,208,128]{2,1,0:T(8,128)(2,1)S(1)} %all-to-all-done.2.recv_ref, bf16[4,4,96,128]{3,2,1,0:T(8,128)(2,1)S(1)} %all_gather.6.tiles_ref), custom_call_target="tpu_custom_call" | custom-call | tf_op jit(solution)/shard_map/pallas_call | solution.py:521
  41.4 3.5 %all-to-all-start.3 = ((bf16[8,208,128]{2,1,0:T(8,128)(2,1)}), bf16[8,208,128]{2,1,0:T(8,128)(2,1)S(1)}, u32[]{:S(2)}, u32[]{:S(2)}) async-start(bf16[8,208,128]{2,1,0:T(8,128)(2,1)} %get-tuple-element.143), calls=%async_computation.4 | async-start | bytes 851968 | tf_op jit(solution)/shard_map/all_to_all | solution.py:531
  44.9 0.1 slice.79
  45.0 0.1 pad_maximum_fusion.2
  45.0 0.6 reverse.1
  45.7 0.1 slice.161
  45.8 0.1 concatenate.20
  45.9 0.1 broadcast_in_dim.161.line_ref
  45.9 7.5 %shard_map.104.mat_ref = bf16[8,2176,256]{2,1,0:T(8,128)(2,1)} custom-call(f32[8,1,2304]{2,1,0:T(1,128)S(1)} %broadcast_in_dim.161.line_ref), custom_call_target="tpu_custom_call" | custom-call | tf_op jit(solution)/shard_map/pallas_call | solution.py:512
  53.4 3.8 %all-to-all-done.3.recv_ref = bf16[8,208,128]{2,1,0:T(8,128)(2,1)S(1)} async-done(((bf16[8,208,128]{2,1,0:T(8,128)(2,1)}), bf16[8,208,128]{2,1,0:T(8,128)(2,1)S(1)}, u32[]{:S(2)}, u32[]{:S(2)}) %all-to-all-start.3) | async-done | bytes 426016 | tf_op jit(solution)/shard_map/all_to_all | solution.py:531
  57.1 9.3 %shard_map.105.filt_ref = f32[8,128,128]{2,1,0:T(8,128)S(1)} custom-call(bf16[8,208,128]{2,1,0:T(8,128)(2,1)S(1)} %all-to-all-done.3.recv_ref, bf16[8,2176,256]{2,1,0:T(8,128)(2,1)} %shard_map.104.mat_ref), custom_call_target="tpu_custom_call" | custom-call | tf_op jit(solution)/shard_map/pallas_call | solution.py:534
  66.4 0.0 copy-start
  66.5 11.8 %shard_map.106 = (f32[2,4,96,128]{3,2,1,0:T(8,128)S(1)}, bf16[2,4,96,128]{3,2,1,0:T(8,128)(2,1)S(1)}) custom-call(s32[1]{0:T(128)} %bitcast.73.core_ref, f32[6,192,128]{2,1,0:T(8,128)S(1)} %get-tuple-element.140.fields_ref, f32[192,8]{1,0:T(8,128)S(1)} %get-tuple-element.141.ids_ref, f32[24,128]{1,0:T(8,128)S(1)} %get-tuple-element.142.seg_ref, ...), custom_call_target="tpu_custom_call" | custom-call | tf_op jit(solution)/shard_map/pallas_call | solution.py:549
  78.3 0.1 collective-permute-start.2
  78.4 1.4 %collective-permute-done.2 = bf16[2,4,96,128]{3,2,1,0:T(8,128)(2,1)S(1)} collective-permute-done((bf16[2,4,96,128]{3,2,1,0:T(8,128)(2,1)S(1)}, bf16[2,4,96,128]{3,2,1,0:T(8,128)(2,1)S(1)}, u32[]{:S(2)}, u32[]{:S(2)}) %collective-permute-start.2) | collective-permute-done | bytes 196640 | tf_op jit(solution)/shard_map/ppermute | solution.py:560
  79.8 1.2 %collective-permute-start.3 = (bf16[4,96,128]{2,1,0:T(8,128)(2,1)S(1)}, bf16[4,96,128]{2,1,0:T(8,128)(2,1)S(1)}, u32[]{:S(2)}, u32[]{:S(2)}) collective-permute-start(bf16[4,96,128]{2,1,0:T(8,128)(2,1)S(1)} %fusion.68), channel_id=1, source_target_pairs={{0,16},{8,24},{16,0},{24,8},{1,17},{9,25},{17,1},{25,9},{2,18},{10... | collective-permute-start | bytes 294920 | tf_op jit(solution)/shard_map/ppermute | solution.py:569
  81.1 3.7 %collective-permute-done.3 = bf16[4,96,128]{2,1,0:T(8,128)(2,1)S(1)} collective-permute-done((bf16[4,96,128]{2,1,0:T(8,128)(2,1)S(1)}, bf16[4,96,128]{2,1,0:T(8,128)(2,1)S(1)}, u32[]{:S(2)}, u32[]{:S(2)}) %collective-permute-start.3) | collective-permute-done | bytes 98336 | tf_op jit(solution)/shard_map/ppermute | solution.py:569
  84.8 0.5 slice.106
  86.7 0.9 conditional.1
  86.9 0.7 copy.168
  (22 shorter events, 0.1 us)
Async XLA Ops:
  6.5 38.3 %copy-start.3 = (f32[8,1025]{1,0:T(8,128)S(1)}, f32[8,1025]{1,0:T(8,128)}, u32[]{:S(2)}) copy-start(f32[8,1025]{1,0:T(8,128)} %param.27) | copy-start | bytes 98404
  8.9 19.7 %all-to-all-start.2 = ((bf16[8,208,128]{2,1,0:T(8,128)(2,1)}), bf16[8,208,128]{2,1,0:T(8,128)(2,1)S(1)}, u32[]{:S(2)}, u32[]{:S(2)}) async-start(bf16[8,208,128]{2,1,0:T(8,128)(2,1)} %shard_map.102), calls=%async_computation.3 | async-start | bytes 851968 | tf_op jit(solution)/shard_map/all_to_all | solution.py:498
  41.4 15.7 %all-to-all-start.3 = ((bf16[8,208,128]{2,1,0:T(8,128)(2,1)}), bf16[8,208,128]{2,1,0:T(8,128)(2,1)S(1)}, u32[]{:S(2)}, u32[]{:S(2)}) async-start(bf16[8,208,128]{2,1,0:T(8,128)(2,1)} %get-tuple-element.143), calls=%async_computation.4 | async-start | bytes 851968 | tf_op jit(solution)/shard_map/all_to_all | solution.py:531
  66.4 20.2 %copy-start = (s32[8,2048]{1,0:T(8,128)S(1)}, s32[8,2048]{1,0:T(8,128)}, u32[]{:S(2)}) copy-start(s32[8,2048]{1,0:T(8,128)} %r_ref.1) | copy-start | bytes 196612
  66.4 20.2 %copy-start.1 = (s32[8,2048]{1,0:T(8,128)S(1)}, s32[8,2048]{1,0:T(8,128)}, u32[]{:S(2)}) copy-start(s32[8,2048]{1,0:T(8,128)} %c_ref.1) | copy-start | bytes 196612
  66.4 20.2 %copy-start.2 = (f32[8,2048]{1,0:T(8,128)S(1)}, f32[8,2048]{1,0:T(8,128)}, u32[]{:S(2)}) copy-start(f32[8,2048]{1,0:T(8,128)} %ang_ref.1) | copy-start | bytes 196612
  66.4 20.2 %copy-start.4 = (bf16[8,2048]{1,0:T(8,128)(2,1)S(1)}, bf16[8,2048]{1,0:T(8,128)(2,1)}, u32[]{:S(2)}) copy-start(bf16[8,2048]{1,0:T(8,128)(2,1)} %fr_ref.1) | copy-start | bytes 98308
  66.4 20.2 %copy-start.5 = (bf16[8,2048]{1,0:T(8,128)(2,1)S(1)}, bf16[8,2048]{1,0:T(8,128)(2,1)}, u32[]{:S(2)}) copy-start(bf16[8,2048]{1,0:T(8,128)(2,1)} %fc_ref.1) | copy-start | bytes 98308
  66.5 20.2 %copy-start.6 = (s32[8,16]{1,0:T(8,128)S(1)}, s32[8,16]{1,0:T(8,128)}, u32[]{:S(2)}) copy-start(s32[8,16]{1,0:T(8,128)} %slot_ref.1) | copy-start | bytes 1540
  66.5 20.2 %copy-start.7 = (s32[1,1,32]{2,1,0:T(1,128)S(1)}, s32[1,1,32]{2,1,0:T(1,128)}, u32[]{:S(2)}) copy-start(s32[1,1,32]{2,1,0:T(1,128)} %param.20) | copy-start | bytes 388
  66.5 20.2 %copy-start.8 = (s32[32]{0:T(128)S(1)}, s32[32]{0:T(128)}, u32[]{:S(2)}) copy-start(s32[32]{0:T(128)} %th_ref.1) | copy-start | bytes 388
  78.3 1.5 %collective-permute-start.2 = (bf16[2,4,96,128]{3,2,1,0:T(8,128)(2,1)S(1)}, bf16[2,4,96,128]{3,2,1,0:T(8,128)(2,1)S(1)}, u32[]{:S(2)}, u32[]{:S(2)}) collective-permute-start(bf16[2,4,96,128]{3,2,1,0:T(8,128)(2,1)S(1)} %get-tuple-element.145), channel_id=1, source_target_pairs={{0,8},{8,0},{16,24},{24,16},{1,9},{9,1},{17,25},{25,17},{2,10},{10... | collective-permute-start | bytes 589832 | tf_op jit(solution)/shard_map/ppermute | solution.py:560
  79.8 4.9 %collective-permute-start.3 = (bf16[4,96,128]{2,1,0:T(8,128)(2,1)S(1)}, bf16[4,96,128]{2,1,0:T(8,128)(2,1)S(1)}, u32[]{:S(2)}, u32[]{:S(2)}) collective-permute-start(bf16[4,96,128]{2,1,0:T(8,128)(2,1)S(1)} %fusion.68), channel_id=1, source_target_pairs={{0,16},{8,24},{16,0},{24,8},{1,17},{9,25},{17,1},{25,9},{2,18},{10... | collective-permute-start | bytes 294920 | tf_op jit(solution)/shard_map/ppermute | solution.py:569
where the time goes:
time: 94.5 us; the launch traced here: 94.4 us
  Pallas kernels  43.7 us (46%)
  between operations  14.9 us (16%)
  waiting for transfers between devices  14.6 us (15%)
  starting transfers between devices  12 us (13%)
  blocking collectives  6.65 us (7%)
  local copies, waits for them, and re-layouts  2.17 us (2%)
    pallas_call x1, Pallas kernels, body(): call(functools.partial(project_kernel, cap, kept), (jax.ShapeDtypeStruct(...  12.9 us
    pallas_call x1, Pallas kernels, body(): call(functools.partial(back_kernel, blocks), (jax.ShapeDtypeStruct((pairs...  11.8 us
    pallas_call x1, Pallas kernels, body(): call(functools.partial(filter_kernel, kept, blocks), jax.ShapeDtypeStruct...  9.25 us
    pallas_call x1, Pallas kernels, body(): call(toeplitz_kernel, jax.ShapeDtypeStruct((dets, spans * width, 2 * widt...  7.45 us
    all_to_all x1, starting transfers between devices, body(): recv = lax.all_to_all(packed, 'tm', split_axis=0, concat_axis=0, tiled=True)  7.28 us
    all_gather x1, blocking collectives, body(): lax.all_gather(sky_map.reshape(tile_dev, 3 * part, side), 'det', axis=0)  6.65 us
    all_to_all x1, waiting for transfers between devices, body(): recv = lax.all_to_all(packed, 'tm', split_axis=0, concat_axis=0, tiled=True)  5.72 us
    all_to_all x1, waiting for transfers between devices, body(): heard = lax.all_to_all(sent, 'tm', split_axis=0, concat_axis=0, tiled=True)  3.75 us
  transfers between devices with their start and end apart: 4, of which 4 were waited for; matrix products, arithmetic and copies ran while one was open for 1% of the time, Pallas kernels for 8%

commit v1 on v0

--- a/solution.py
+++ b/solution.py
@@ -403,7 +403,9 @@
         - 1
     )
     served_slot = lax.all_to_all(asked_slot, "tm", split_axis=0, concat_axis=0, tiled=True)
-    every_tile = lax.all_gather(owned_tiles, "tm", axis=0, tiled=True)
+    every_tile = jnp.broadcast_to(owned_tiles[None], (owner_total,) + owned_tiles.shape)
+    every_tile = lax.all_to_all(every_tile, "tm", split_axis=0, concat_axis=0)
+    every_tile = every_tile.reshape((owner_total * tile_dev,) + owned_tiles.shape[1:])
     listed = jnp.take(every_tile, position, axis=0)
     det_local, time_local = hit_row.shape
     run_length = time_local // run_slot.shape[1]
@@ -458,7 +460,9 @@
             for slot_id in range(tile_dev)
         ]
     )
-    return lax.psum_scatter(summed, "det", scatter_dimension=2, tiled=True)
+    summed = summed.reshape(tile_dev, 3, groups_det, part, side_len)
+    shares = lax.all_to_all(summed, "det", split_axis=2, concat_axis=0)
+    return jnp.sum(shares.reshape(groups_det, tile_dev, 3, part, side_len), axis=0)
 
 
 def body(

time: 94.5 us -> 81.4 us (0.86)
  between operations: 14.9 us -> 1.56 us
  waiting for transfers between devices: 14.6 us -> 17 us
  starting transfers between devices: 12 us -> 10.9 us
    all_to_all x1, waiting for transfers between devices: 3.75 us -> 5.01 us  [body(): heard = lax.all_to_all(sent, 'tm', split_axis=0, concat_axis=0, tiled=True)]
    ppermute x1, starting transfers between devices: 1.23 us -> 0.07 us  [body(): lax.ppermute(of_pair(lax.rem(half + step, pairs)).astype(bf16), 'det', ring)]
    ppermute x1, waiting for transfers between devices: 3.67 us -> 4.82 us  [body(): lax.ppermute(of_pair(lax.rem(half + step, pairs)).astype(bf16), 'det', ring)]
  transfers between devices with their start and end apart: 4 -> 4, of which waited for: 4 -> 4; matrix products, arithmetic and copies ran while one was open for 1% -> 1% of each run, Pallas kernels for 8% -> 9%
where the time goes in v1:
time: 81.4 us; the launch traced here: 81.7 us
  Pallas kernels  43.1 us (53%)
  waiting for transfers between devices  17 us (21%)
  starting transfers between devices  10.9 us (13%)
  blocking collectives  6.65 us (8%)
  local copies, waits for them, and re-layouts  2.17 us (3%)
  between operations  1.56 us (2%)
    pallas_call x1, Pallas kernels, body(): call(functools.partial(project_kernel, cap, kept), (jax.ShapeDtypeStruct(...  12.6 us
    pallas_call x1, Pallas kernels, body(): call(functools.partial(back_kernel, blocks), (jax.ShapeDtypeStruct((pairs...  11.5 us
    pallas_call x1, Pallas kernels, body(): call(functools.partial(filter_kernel, kept, blocks), jax.ShapeDtypeStruct...  9.26 us
    pallas_call x1, Pallas kernels, body(): call(toeplitz_kernel, jax.ShapeDtypeStruct((dets, spans * width, 2 * widt...  7.45 us
    all_to_all x1, starting transfers between devices, body(): recv = lax.all_to_all(packed, 'tm', split_axis=0, concat_axis=0, tiled=True)  7.29 us
    all_gather x1, blocking collectives, body(): lax.all_gather(sky_map.reshape(tile_dev, 3 * part, side), 'det', axis=0)  6.65 us
    all_to_all x1, waiting for transfers between devices, body(): recv = lax.all_to_all(packed, 'tm', split_axis=0, concat_axis=0, tiled=True)  5.72 us
    all_to_all x1, waiting for transfers between devices, body(): heard = lax.all_to_all(sent, 'tm', split_axis=0, concat_axis=0, tiled=True)  5.01 us
  transfers between devices with their start and end apart: 4, of which 4 were waited for; matrix products, arithmetic and copies ran while one was open for 1% of the time, Pallas kernels for 9%

profile of v1, /device:TPU:0, one launch (start us, length us, event | category | flops | bytes accessed | tf_op | source)
XLA Modules:
  0.0 81.7 jit_solution(15180994667871369946)
XLA Ops:
  0.0 2.3 %shard_map.102 = bf16[8,208,128]{2,1,0:T(8,128)(2,1)} custom-call(s32[32]{0:T(128)} %bitcast.272, s32[32]{0:T(128)} %th_ref.1, s32[8,16]{1,0:T(8,128)} %slot_ref.1, s32[8,2048]{1,0:T(8,128)} %r_ref.1, s32[8,2048]{1,0:T(8,128)} %c_ref.1, bf16[8,2048]{1,0:T(8,128)(2,1)} %fr_ref.1, bf16[8,2048]{1,0:T(8,128)(2,1)} %fc_ref.1, f32[8,2048]{1,0:T(8,128)} %ang_ref.1), custom_call_target="tpu_custom_call" | custom-call | tf_op jit(solution)/shard_map/pallas_call | solution.py:495
  2.3 7.3 %all-to-all-start.4 = ((bf16[8,208,128]{2,1,0:T(8,128)(2,1)}), bf16[8,208,128]{2,1,0:T(8,128)(2,1)S(1)}, u32[]{:S(2)}, u32[]{:S(2)}) async-start(bf16[8,208,128]{2,1,0:T(8,128)(2,1)} %shard_map.102), calls=%async_computation.4 | async-start | bytes 851968 | tf_op jit(solution)/shard_map/all_to_all | solution.py:502
  9.6 6.7 %all_gather.3.tiles_ref = bf16[4,4,96,128]{3,2,1,0:T(8,128)(2,1)S(1)} all-gather(bf16[1,4,96,128]{3,2,1,0:T(8,128)(2,1)} %bitcast.271), channel_id=1, replica_groups=mesh['det'=4,'tm'=8] {'det'}, dimensions={0}, use_global_device_ids=true | all-gather | bytes 491520 | tf_op jit(solution)/shard_map/all_gather | solution.py:503
  16.3 5.7 %all-to-all-done.4.recv_ref = bf16[8,208,128]{2,1,0:T(8,128)(2,1)S(1)} async-done(((bf16[8,208,128]{2,1,0:T(8,128)(2,1)}), bf16[8,208,128]{2,1,0:T(8,128)(2,1)S(1)}, u32[]{:S(2)}, u32[]{:S(2)}) %all-to-all-start.4) | async-done | bytes 426016 | tf_op jit(solution)/shard_map/all_to_all | solution.py:502
  22.0 12.6 %shard_map.103 = (bf16[8,208,128]{2,1,0:T(8,128)(2,1)}, f32[6,192,128]{2,1,0:T(8,128)S(1)}, f32[192,8]{1,0:T(8,128)S(1)}, f32[24,128]{1,0:T(8,128)S(1)}) custom-call(bf16[8,208,128]{2,1,0:T(8,128)(2,1)S(1)} %all-to-all-done.4.recv_ref, bf16[4,4,96,128]{3,2,1,0:T(8,128)(2,1)S(1)} %all_gather.3.tiles_ref), custom_call_target="tpu_custom_call" | custom-call | tf_op jit(solution)/shard_map/pallas_call | solution.py:525
  34.5 3.5 %all-to-all-start.5 = ((bf16[8,208,128]{2,1,0:T(8,128)(2,1)}), bf16[8,208,128]{2,1,0:T(8,128)(2,1)S(1)}, u32[]{:S(2)}, u32[]{:S(2)}) async-start(bf16[8,208,128]{2,1,0:T(8,128)(2,1)} %get-tuple-element.143), calls=%async_computation.5 | async-start | bytes 851968 | tf_op jit(solution)/shard_map/all_to_all | solution.py:535
  38.0 0.1 slice.79
  38.1 0.1 pad_maximum_fusion.2
  38.2 0.6 reverse.1
  38.8 0.1 slice.161
  38.9 0.1 concatenate.21
  39.0 0.1 broadcast_in_dim.168.line_ref
  39.1 7.5 %shard_map.104.mat_ref = bf16[8,2176,256]{2,1,0:T(8,128)(2,1)} custom-call(f32[8,1,2304]{2,1,0:T(1,128)S(1)} %broadcast_in_dim.168.line_ref), custom_call_target="tpu_custom_call" | custom-call | tf_op jit(solution)/shard_map/pallas_call | solution.py:516
  46.5 5.0 %all-to-all-done.5.recv_ref = bf16[8,208,128]{2,1,0:T(8,128)(2,1)S(1)} async-done(((bf16[8,208,128]{2,1,0:T(8,128)(2,1)}), bf16[8,208,128]{2,1,0:T(8,128)(2,1)S(1)}, u32[]{:S(2)}, u32[]{:S(2)}) %all-to-all-start.5) | async-done | bytes 426016 | tf_op jit(solution)/shard_map/all_to_all | solution.py:535
  51.5 9.3 %shard_map.105.filt_ref = f32[8,128,128]{2,1,0:T(8,128)S(1)} custom-call(bf16[8,208,128]{2,1,0:T(8,128)(2,1)S(1)} %all-to-all-done.5.recv_ref, bf16[8,2176,256]{2,1,0:T(8,128)(2,1)} %shard_map.104.mat_ref), custom_call_target="tpu_custom_call" | custom-call | tf_op jit(solution)/shard_map/pallas_call | solution.py:538
  60.8 0.0 copy-start.2
  60.9 11.5 %shard_map.106 = (f32[2,4,96,128]{3,2,1,0:T(8,128)S(1)}, bf16[2,4,96,128]{3,2,1,0:T(8,128)(2,1)S(1)}) custom-call(s32[1]{0:T(128)} %bitcast.74.core_ref, f32[6,192,128]{2,1,0:T(8,128)S(1)} %get-tuple-element.140.fields_ref, f32[192,8]{1,0:T(8,128)S(1)} %get-tuple-element.141.ids_ref, f32[24,128]{1,0:T(8,128)S(1)} %get-tuple-element.142.seg_ref, ...), custom_call_target="tpu_custom_call" | custom-call | tf_op jit(solution)/shard_map/pallas_call | solution.py:553
  72.4 0.1 collective-permute-start.2
  72.5 1.4 %collective-permute-done.2 = bf16[2,4,96,128]{3,2,1,0:T(8,128)(2,1)S(1)} collective-permute-done((bf16[2,4,96,128]{3,2,1,0:T(8,128)(2,1)S(1)}, bf16[2,4,96,128]{3,2,1,0:T(8,128)(2,1)S(1)}, u32[]{:S(2)}, u32[]{:S(2)}) %collective-permute-start.2) | collective-permute-done | bytes 196640 | tf_op jit(solution)/shard_map/ppermute | solution.py:564
  73.9 0.1 collective-permute-start.3
  74.0 4.8 %collective-permute-done.3 = bf16[4,96,128]{2,1,0:T(8,128)(2,1)S(1)} collective-permute-done((bf16[4,96,128]{2,1,0:T(8,128)(2,1)S(1)}, bf16[4,96,128]{2,1,0:T(8,128)(2,1)S(1)}, u32[]{:S(2)}, u32[]{:S(2)}) %collective-permute-start.3) | collective-permute-done | bytes 98336 | tf_op jit(solution)/shard_map/ppermute | solution.py:573
  78.9 0.5 slice.106
  80.8 0.2 conditional.1
  81.0 0.7 copy-done.3
  (23 shorter events, 0.1 us)
Async XLA Ops:
  0.0 38.0 %copy-start.4 = (f32[8,1025]{1,0:T(8,128)S(1)}, f32[8,1025]{1,0:T(8,128)}, u32[]{:S(2)}) copy-start(f32[8,1025]{1,0:T(8,128)} %param.27) | copy-start | bytes 98404
  2.3 19.7 %all-to-all-start.4 = ((bf16[8,208,128]{2,1,0:T(8,128)(2,1)}), bf16[8,208,128]{2,1,0:T(8,128)(2,1)S(1)}, u32[]{:S(2)}, u32[]{:S(2)}) async-start(bf16[8,208,128]{2,1,0:T(8,128)(2,1)} %shard_map.102), calls=%async_computation.4 | async-start | bytes 851968 | tf_op jit(solution)/shard_map/all_to_all | solution.py:502
  34.5 17.0 %all-to-all-start.5 = ((bf16[8,208,128]{2,1,0:T(8,128)(2,1)}), bf16[8,208,128]{2,1,0:T(8,128)(2,1)S(1)}, u32[]{:S(2)}, u32[]{:S(2)}) async-start(bf16[8,208,128]{2,1,0:T(8,128)(2,1)} %get-tuple-element.143), calls=%async_computation.5 | async-start | bytes 851968 | tf_op jit(solution)/shard_map/all_to_all | solution.py:535
  60.8 19.9 %copy-start = (s32[8,2048]{1,0:T(8,128)S(1)}, s32[8,2048]{1,0:T(8,128)}, u32[]{:S(2)}) copy-start(s32[8,2048]{1,0:T(8,128)} %r_ref.1) | copy-start | bytes 196612
  60.8 19.9 %copy-start.1 = (s32[8,2048]{1,0:T(8,128)S(1)}, s32[8,2048]{1,0:T(8,128)}, u32[]{:S(2)}) copy-start(s32[8,2048]{1,0:T(8,128)} %c_ref.1) | copy-start | bytes 196612
  60.8 19.9 %copy-start.2 = (f32[8,2048]{1,0:T(8,128)S(1)}, f32[8,2048]{1,0:T(8,128)}, u32[]{:S(2)}) copy-start(f32[8,2048]{1,0:T(8,128)} %ang_ref.1) | copy-start | bytes 196612
  60.8 19.9 %copy-start.5 = (bf16[8,2048]{1,0:T(8,128)(2,1)S(1)}, bf16[8,2048]{1,0:T(8,128)(2,1)}, u32[]{:S(2)}) copy-start(bf16[8,2048]{1,0:T(8,128)(2,1)} %fr_ref.1) | copy-start | bytes 98308
  60.9 19.9 %copy-start.6 = (bf16[8,2048]{1,0:T(8,128)(2,1)S(1)}, bf16[8,2048]{1,0:T(8,128)(2,1)}, u32[]{:S(2)}) copy-start(bf16[8,2048]{1,0:T(8,128)(2,1)} %fc_ref.1) | copy-start | bytes 98308
  60.9 19.9 %copy-start.7 = (s32[8,16]{1,0:T(8,128)S(1)}, s32[8,16]{1,0:T(8,128)}, u32[]{:S(2)}) copy-start(s32[8,16]{1,0:T(8,128)} %slot_ref.1) | copy-start | bytes 1540
  60.9 19.9 %copy-start.8 = (s32[1,1,32]{2,1,0:T(1,128)S(1)}, s32[1,1,32]{2,1,0:T(1,128)}, u32[]{:S(2)}) copy-start(s32[1,1,32]{2,1,0:T(1,128)} %param.20) | copy-start | bytes 388
  60.9 19.9 %copy-start.9 = (s32[32]{0:T(128)S(1)}, s32[32]{0:T(128)}, u32[]{:S(2)}) copy-start(s32[32]{0:T(128)} %th_ref.1) | copy-start | bytes 388
  72.4 1.5 %collective-permute-start.2 = (bf16[2,4,96,128]{3,2,1,0:T(8,128)(2,1)S(1)}, bf16[2,4,96,128]{3,2,1,0:T(8,128)(2,1)S(1)}, u32[]{:S(2)}, u32[]{:S(2)}) collective-permute-start(bf16[2,4,96,128]{3,2,1,0:T(8,128)(2,1)S(1)} %get-tuple-element.145), channel_id=1, source_target_pairs={{0,8},{8,0},{16,24},{24,16},{1,9},{9,1},{17,25},{25,17},{2,10},{10... | collective-permute-start | bytes 589832 | tf_op jit(solution)/shard_map/ppermute | solution.py:564
  73.9 4.9 %collective-permute-start.3 = (bf16[4,96,128]{2,1,0:T(8,128)(2,1)S(1)}, bf16[4,96,128]{2,1,0:T(8,128)(2,1)S(1)}, u32[]{:S(2)}, u32[]{:S(2)}) collective-permute-start(bf16[4,96,128]{2,1,0:T(8,128)(2,1)S(1)} %fusion.68), channel_id=1, source_target_pairs={{0,16},{8,24},{16,0},{24,8},{1,17},{9,25},{17,1},{25,9},{2,18},{10... | collective-permute-start | bytes 294920 | tf_op jit(solution)/shard_map/ppermute | solution.py:573
  81.0 0.7 copy-start.3

commit v2 on v1

--- a/solution.py
+++ b/solution.py
@@ -91,8 +91,9 @@
 
 
 GROUP = 4
+UNROLL = 4
 META = 16
-VMEM_LIMIT = 48 * 1024 * 1024
+VMEM_LIMIT = 40 * 1024 * 1024
 f32 = jnp.float32
 bf16 = jnp.bfloat16
 
@@ -171,10 +172,26 @@
     out_ref[:, len(fields) * cap :, :] = meta_ref[...].astype(bf16)
 
 
-def weights_of(index, high, shape):
-    rows = iota(shape, 0)
-    low = (1.0 - high).astype(bf16).astype(f32)
-    return jnp.where(rows == index, low, jnp.where(rows == index + 1, high, 0.0))
+def weights_of(fields_ref, axis, run, shape):
+    index, high, low = (
+        fields_ref[f + axis, pl.ds(run, 1), :].astype(bf16) for f in (0, 2, 6)
+    )
+    rows = iota(shape, 0).astype(f32).astype(bf16)
+    zero = jnp.zeros((), bf16)
+    return jnp.where(rows == index, low, jnp.where(rows == index + 1, high, zero))
+
+
+def segments(seg_ref, tile_dev):
+    return [
+        jnp.max(seg_ref[8 + tile : 9 + tile, :]).astype(jnp.int32) // GROUP for tile in range(tile_dev)
+    ]
+
+
+def tile_of(group, ends):
+    tile = jnp.int32(0)
+    for end in ends[:-1]:
+        tile = tile + (group >= end).astype(jnp.int32)
+    return tile
 
 
 def project_kernel(
@@ -230,39 +247,38 @@
         fields_ref[f] = sorted_fields[f]
     fields_ref[4] = jnp.cos(twice)
     fields_ref[5] = jnp.sin(twice)
+    fields_ref[6] = (1.0 - sorted_fields[2]).astype(bf16).astype(f32)
+    fields_ref[7] = (1.0 - sorted_fields[3]).astype(bf16).astype(f32)
     sig_ref[...] = jnp.zeros_like(sig_ref)
-    for tile in range(tile_dev):
+    ends = segments(seg_ref, tile_dev)
+
+    def one_group(group):
+        tile = tile_of(group, ends)
         rows = jnp.concatenate([tiles_ref[d, tile] for d in range(groups_det)], axis=0)
-        first = jnp.max(start[tile : tile + 1, :]).astype(jnp.int32) // GROUP
-        last = jnp.max(stop[tile : tile + 1, :]).astype(jnp.int32) // GROUP
-
-        def step(g, carry, rows=rows):
-            base = g * GROUP
-            cols = []
-            for k in range(GROUP):
-                c = fields_ref[1, pl.ds(base + k, 1), :].astype(jnp.int32)
-                fc = fields_ref[3, pl.ds(base + k, 1), :]
-                cols.append(weights_of(c, fc, (side, width)).astype(bf16))
-            partial_rows = dot_nn(rows, jnp.concatenate(cols, axis=1))
-            for k in range(GROUP):
-                r = fields_ref[0, pl.ds(base + k, 1), :].astype(jnp.int32)
-                fr = fields_ref[2, pl.ds(base + k, 1), :]
-                row_weight = weights_of(r, fr, (side, width))
-                values = []
-                for p in range(3):
-                    total = None
-                    for d in range(groups_det):
-                        at = d * rows_dev + p * part
-                        term = partial_rows[at : at + part, k * width : (k + 1) * width]
-                        term = term * row_weight[d * part : (d + 1) * part]
-                        total = term if total is None else total + term
-                    values.append(jnp.sum(total, axis=0, keepdims=True))
-                cos = fields_ref[4, pl.ds(base + k, 1), :]
-                sin = fields_ref[5, pl.ds(base + k, 1), :]
-                sig_ref[pl.ds(base + k, 1), :] = values[0] + cos * values[1] + sin * values[2]
-            return carry
-
-        lax.fori_loop(first, last, step, 0)
+        base = group * GROUP
+        cols = [weights_of(fields_ref, 1, base + k, (side, width)) for k in range(GROUP)]
+        partial_rows = dot_nn(rows, jnp.concatenate(cols, axis=1))
+        for k in range(GROUP):
+            row_weight = weights_of(fields_ref, 0, base + k, (side, width)).astype(f32)
+            values = []
+            for p in range(3):
+                total = None
+                for d in range(groups_det):
+                    at = d * rows_dev + p * part
+                    term = partial_rows[at : at + part, k * width : (k + 1) * width]
+                    term = term * row_weight[d * part : (d + 1) * part]
+                    total = term if total is None else total + term
+                values.append(jnp.sum(total, axis=0, keepdims=True))
+            cos = fields_ref[4, pl.ds(base + k, 1), :]
+            sin = fields_ref[5, pl.ds(base + k, 1), :]
+            sig_ref[pl.ds(base + k, 1), :] = values[0] + cos * values[1] + sin * values[2]
+
+    def step(g, carry):
+        for u in range(UNROLL):
+            one_group(g * UNROLL + u)
+        return carry
+
+    lax.fori_loop(0, (ends[-1] + UNROLL - 1) // UNROLL, step, 0)
     sent = sig_ref[...].astype(bf16)
     notes = scratch_ref[...].astype(bf16)
 
@@ -275,47 +291,81 @@
 
 
 def toeplitz_kernel(line_ref, out_ref):
-    width = out_ref.shape[2] // 2
-    blocks = out_ref.shape[1] // width
-    for m in range(blocks):
-        at = (blocks - 1 - m) * width
-        piece = jnp.broadcast_to(line_ref[0, :, at : at + 2 * width], (width, 2 * width))
-        block = pltpu.roll(piece, width, 1, stride=1, stride_axis=0)[:, :width]
-        high = block.astype(bf16)
-        out_ref[0, m * width : (m + 1) * width, :width] = high
-        out_ref[0, m * width : (m + 1) * width, width:] = (block - high.astype(f32)).astype(bf16)
-
-
-def filter_kernel(kept, blocks_dev, recv_ref, mat_ref, out_ref, line_ref):
-    det = pl.program_id(0)
-    owners = recv_ref.shape[0]
-    width = recv_ref.shape[2]
+    lines, rows, width = out_ref.shape
+    width = width // 2
+    blocks = rows // width
+
+    def one(d, carry):
+        for m in range(blocks):
+            at = (blocks - 1 - m) * width
+            piece = jnp.broadcast_to(line_ref[d, :, at : at + 2 * width], (width, 2 * width))
+            block = pltpu.roll(piece, width, 1, stride=1, stride_axis=0)[:, :width]
+            high = block.astype(bf16)
+            out_ref[d, m * width : (m + 1) * width, :width] = high
+            out_ref[d, m * width : (m + 1) * width, width:] = (block - high.astype(f32)).astype(bf16)
+        return carry
+
+    lax.fori_loop(0, lines, one, 0)
+
+
+def filter_lines(blocks_dev, kept, recv_ref, mat_ref, filt_ref, line_ref):
+    owners, rows, width = recv_ref.shape
+    lines, padded, _ = line_ref.shape
     count = owners * blocks_dev
-    spans = mat_ref.shape[1] // width
-    edge = spans // 2
+    edge = (padded - count) // 2
+    spans = padded - count + 1
+    together = math.gcd(owners, 8)
     line_ref[...] = jnp.zeros_like(line_ref)
-    rows = iota((count, kept), 0)
-
-    def one(o, carry):
-        notes = recv_ref[o, kept:, :].astype(f32)
-        notes = jnp.concatenate([notes[q * 8 : q * 8 + 8] for q in range(notes.shape[0] // 8)], axis=1)[:, :kept]
-        at = notes[3:4] * blocks_dev + notes[1:2]
-        mine = jnp.logical_and(notes[0:1] > 0.5, notes[2:3] == det.astype(f32))
-        at = jnp.where(mine, at, -1.0).astype(jnp.int32)
-        line_ref[edge : edge + count, :] += dot_nn(ones_where(rows == at), recv_ref[o, 0:kept, :])
-        return carry
-
-    lax.fori_loop(0, owners, one, 0, unroll=owners <= 8)
-    spread = jnp.concatenate([line_ref[m : m + count, :].astype(bf16) for m in range(spans)], axis=1)
-    both = dot_nn(spread, mat_ref[0])
-    out_ref[0] = both[:, :width] + both[:, width:]
+
+    def some(first, lines_now, line0):
+        at, values = [], []
+        for o in range(together):
+            notes = recv_ref[first + o, kept:, :].astype(f32)
+            notes = [notes[q * 8 : q * 8 + 8] for q in range(notes.shape[0] // 8)]
+            notes = jnp.concatenate(notes, axis=1)[:, :kept]
+            row = notes[2:3] * count + notes[3:4] * blocks_dev + notes[1:2]
+            at.append(jnp.where(notes[0:1] > 0.5, row, -1.0))
+            values.append(recv_ref[first + o, 0:kept, :])
+        at = jnp.concatenate(at, axis=1).astype(jnp.int32) - line0 * count
+        place = ones_where(iota((lines_now * count, together * kept), 0) == at)
+        return dot_nn(place, jnp.concatenate(values, axis=0))
+
+    if together == owners:
+        found = some(0, lines, 0)
+        for d in range(lines):
+            line_ref[d, edge : edge + count, :] = found[d * count : (d + 1) * count]
+    else:
+
+        def one(g, carry):
+            for d in range(lines):
+                line_ref[d, edge : edge + count, :] += some(g * together, 1, d)
+            return carry
+
+        lax.fori_loop(0, owners // together, one, 0)
+    for d in range(lines):
+        spread = jnp.concatenate([line_ref[d, m : m + count, :].astype(bf16) for m in range(spans)], axis=1)
+        both = dot_nn(spread, mat_ref[d])
+        filt_ref[d] = both[:, :width] + both[:, width:]
 
 
 def back_kernel(
-    blocks_dev, core_ref, fields_ref, ids_ref, seg_ref, filt_ref, mine_ref, theirs_ref, scaled_ref, acc_ref
+    blocks_dev,
+    core_ref,
+    recv_ref,
+    mat_ref,
+    fields_ref,
+    ids_ref,
+    seg_ref,
+    mine_ref,
+    theirs_ref,
+    filt_ref,
+    line_ref,
+    scaled_ref,
+    acc_ref,
 ):
     width = fields_ref.shape[2]
     kept = fields_ref.shape[1]
+    filter_lines(blocks_dev, kept, recv_ref, mat_ref, filt_ref, line_ref)
     pairs, tile_dev, rows_dev, side = mine_ref.shape
     part = rows_dev // 3
     core = core_ref[0]
@@ -334,36 +384,31 @@
     scaled_ref[0] = filtered
     scaled_ref[1] = filtered * fields_ref[4]
     scaled_ref[2] = filtered * fields_ref[5]
+    ends = segments(seg_ref, tile_dev)
+    acc_ref[...] = jnp.zeros_like(acc_ref)
+
+    def one_group(group):
+        base = group * GROUP
+        cols, terms = [], []
+        for k in range(GROUP):
+            cols.append(weights_of(fields_ref, 1, base + k, (side, width)))
+            row_weight = weights_of(fields_ref, 0, base + k, (side, width)).astype(f32)
+            scaled = [scaled_ref[p, pl.ds(base + k, 1), :] for p in range(3)]
+            terms.append(jnp.concatenate([(x * row_weight).astype(bf16) for x in scaled], axis=0))
+        return dot_nt(jnp.concatenate(terms, axis=1), jnp.concatenate(cols, axis=1))
+
+    def step(g, carry):
+        for u in range(UNROLL):
+            acc_ref[tile_of(g * UNROLL + u, ends)] += one_group(g * UNROLL + u)
+        return carry
+
+    lax.fori_loop(0, (ends[-1] + UNROLL - 1) // UNROLL, step, 0)
     for tile in range(tile_dev):
-        first = jnp.max(seg_ref[tile : tile + 1, :]).astype(jnp.int32) // GROUP
-        last = jnp.max(seg_ref[8 + tile : 9 + tile, :]).astype(jnp.int32) // GROUP
-        acc_ref[...] = jnp.zeros_like(acc_ref)
-
-        def step(g, carry):
-            base = g * GROUP
-            cols, terms = [], []
-            for k in range(GROUP):
-                c = fields_ref[1, pl.ds(base + k, 1), :].astype(jnp.int32)
-                fc = fields_ref[3, pl.ds(base + k, 1), :]
-                cols.append(weights_of(c, fc, (side, width)).astype(bf16))
-                r = fields_ref[0, pl.ds(base + k, 1), :].astype(jnp.int32)
-                fr = fields_ref[2, pl.ds(base + k, 1), :]
-                row_weight = weights_of(r, fr, (side, width))
-                terms.append(
-                    jnp.concatenate(
-                        [(scaled_ref[p, pl.ds(base + k, 1), :] * row_weight).astype(bf16) for p in range(3)],
-                        axis=0,
-                    )
-                )
-            acc_ref[...] += dot_nt(jnp.concatenate(terms, axis=1), jnp.concatenate(cols, axis=1))
-            return carry
-
-        lax.fori_loop(first, last, step, 0)
         for h in range(pairs):
             for p in range(3):
                 base = p * side + h * 2 * part
-                mine = acc_ref[pl.ds(pl.multiple_of(base + core * part, part), part), :]
-                theirs = acc_ref[pl.ds(pl.multiple_of(base + (1 - core) * part, part), part), :]
+                mine = acc_ref[tile, pl.ds(pl.multiple_of(base + core * part, part), part), :]
+                theirs = acc_ref[tile, pl.ds(pl.multiple_of(base + (1 - core) * part, part), part), :]
                 mine_ref[h, tile, p * part : (p + 1) * part, :] = mine + poison
                 theirs_ref[h, tile, p * part : (p + 1) * part, :] = (theirs + poison).astype(bf16)
 
@@ -515,10 +560,7 @@
     spans = 2 * (half_band // width) + 1
     matrix = call(
         toeplitz_kernel,
-        jax.ShapeDtypeStruct((dets, spans * width, 2 * width), bf16),
-        grid=(dets,),
-        in_specs=[pl.BlockSpec((1, 1, line.shape[1]), lambda d: (d, 0, 0))],
-        out_specs=pl.BlockSpec((1, spans * width, 2 * width), lambda d: (d, 0, 0)),
+        pltpu.VMEM((dets, spans * width, 2 * width), bf16),
     )(line[:, None, :])
 
     notes = round_up(kept, width) // width * 8
@@ -526,7 +568,7 @@
         functools.partial(project_kernel, cap, kept),
         (
             jax.ShapeDtypeStruct((owners, kept + notes, width), bf16),
-            jax.ShapeDtypeStruct((6, kept, width), f32),
+            jax.ShapeDtypeStruct((8, kept, width), f32),
             jax.ShapeDtypeStruct((kept, 8), f32),
             jax.ShapeDtypeStruct((24, width), f32),
         ),
@@ -535,17 +577,6 @@
     heard = lax.all_to_all(sent, "tm", split_axis=0, concat_axis=0, tiled=True)
 
     count = owners * blocks
-    filtered = call(
-        functools.partial(filter_kernel, kept, blocks),
-        jax.ShapeDtypeStruct((dets, count, width), f32),
-        [pltpu.VMEM((count + spans - 1, width), f32)],
-        grid=(dets,),
-        in_specs=[
-            pl.BlockSpec((owners, kept + notes, width), lambda d: (0, 0, 0)),
-            pl.BlockSpec((1, spans * width, 2 * width), lambda d: (d, 0, 0)),
-        ],
-        out_specs=pl.BlockSpec((1, count, width), lambda d: (d, 0, 0)),
-    )(heard, matrix)
     place = lax.axis_index("det")
     core = lax.rem(place, 2)
     half = lax.div(place, 2)
@@ -556,10 +587,15 @@
             jax.ShapeDtypeStruct((pairs, tile_dev, 3 * part, side), f32),
             jax.ShapeDtypeStruct((pairs, tile_dev, 3 * part, side), bf16),
         ),
-        [pltpu.VMEM((3, kept, width), f32), pltpu.VMEM((3 * side, side), f32)],
-        in_specs=[smem] + [vmem] * 4,
+        [
+            pltpu.VMEM((dets, count, width), f32),
+            pltpu.VMEM((dets, count + spans - 1, width), f32),
+            pltpu.VMEM((3, kept, width), f32),
+            pltpu.VMEM((tile_dev, 3 * side, side), f32),
+        ],
+        in_specs=[smem] + [vmem] * 5,
         out_specs=(vmem, vmem),
-    )(core[None].astype(jnp.int32), fields, ids, seg, filtered)
+    )(core[None].astype(jnp.int32), heard, matrix, fields, ids, seg)
 
     beside = lax.ppermute(theirs, "det", [(i, i ^ 1) for i in range(groups_det)])
 

time: 81.4 us -> 67.6 us (0.83)
  Pallas kernels: 43.1 us -> 24.2 us
  local copies, waits for them, and re-layouts: 2.17 us -> 9.11 us
  waiting for transfers between devices: 17 us -> 12.4 us
  starting transfers between devices: 10.9 us -> 13.1 us
    pallas_call x2 -> x1, Pallas kernels: 16.7 us -> 5.16 us  [body(): call(toeplitz_kernel, pltpu.VMEM((dets, spans * width, 2 * width), bf16))]
    unnamed x22 -> x26, local copies, waits for them, and re-layouts: 1.44 us -> 8.37 us
    pallas_call x1, Pallas kernels: 12.6 us -> 7.18 us  [body(): call(functools.partial(project_kernel, cap, kept), (jax.ShapeDtypeStruct(...]
    all_to_all x1, waiting for transfers between devices: 5.01 us -> 2.21 us  [body(): heard = lax.all_to_all(sent, 'tm', split_axis=0, concat_axis=0, tiled=True)]
    ppermute x1, starting transfers between devices: 0.07 us -> 2.13 us  [body(): lax.ppermute(of_pair(lax.rem(half + step, pairs)).astype(bf16), 'det', ring)]
    pallas_call x1, Pallas kernels: 11.5 us -> 9.54 us  [body(): call(functools.partial(back_kernel, blocks), (jax.ShapeDtypeStruct((pairs...]
    ppermute x1, waiting for transfers between devices: 4.82 us -> 3.1 us  [body(): lax.ppermute(of_pair(lax.rem(half + step, pairs)).astype(bf16), 'det', ring)]
  transfers between devices with their start and end apart: 4 -> 4, of which waited for: 4 -> 4; matrix products, arithmetic and copies ran while one was open for 1% -> 1% of each run, Pallas kernels for 9% -> 8%
where the time goes in v2:
time: 67.6 us; the launch traced here: 67.4 us
  Pallas kernels  24.2 us (36%)
  starting transfers between devices  13.1 us (19%)
  waiting for transfers between devices  12.4 us (18%)
  local copies, waits for them, and re-layouts  9.11 us (13%)
  blocking collectives  6.65 us (10%)
  between operations  1.51 us (2%)
    pallas_call x1, Pallas kernels, body(): call(functools.partial(back_kernel, blocks), (jax.ShapeDtypeStruct((pairs...  9.54 us
    unnamed x26, local copies, waits for them, and re-layouts  8.37 us
    all_to_all x1, starting transfers between devices, body(): recv = lax.all_to_all(packed, 'tm', split_axis=0, concat_axis=0, tiled=True)  7.29 us
    pallas_call x1, Pallas kernels, body(): call(functools.partial(project_kernel, cap, kept), (jax.ShapeDtypeStruct(...  7.18 us
    all_gather x1, blocking collectives, body(): lax.all_gather(sky_map.reshape(tile_dev, 3 * part, side), 'det', axis=0)  6.65 us
    all_to_all x1, waiting for transfers between devices, body(): recv = lax.all_to_all(packed, 'tm', split_axis=0, concat_axis=0, tiled=True)  5.72 us
    pallas_call x1, Pallas kernels, body(): call(toeplitz_kernel, pltpu.VMEM((dets, spans * width, 2 * width), bf16))  5.16 us
    all_to_all x1, starting transfers between devices, body(): heard = lax.all_to_all(sent, 'tm', split_axis=0, concat_axis=0, tiled=True)  3.63 us
  transfers between devices with their start and end apart: 4, of which 4 were waited for; matrix products, arithmetic and copies ran while one was open for 1% of the time, Pallas kernels for 8%

profile of v2, /device:TPU:0, one launch (start us, length us, event | category | flops | bytes accessed | tf_op | source)
XLA Modules:
  0.0 67.4 jit_solution(12297845314031546827)
XLA Ops:
  0.0 2.3 %shard_map.102 = bf16[8,208,128]{2,1,0:T(8,128)(2,1)} custom-call(s32[32]{0:T(128)} %bitcast.272, s32[32]{0:T(128)} %th_ref.1, s32[8,16]{1,0:T(8,128)} %slot_ref.1, s32[8,2048]{1,0:T(8,128)} %r_ref.1, s32[8,2048]{1,0:T(8,128)} %c_ref.1, bf16[8,2048]{1,0:T(8,128)(2,1)} %fr_ref.1, bf16[8,2048]{1,0:T(8,128)(2,1)} %fc_ref.1, f32[8,2048]{1,0:T(8,128)} %ang_ref.1), custom_call_target="tpu_custom_call" | custom-call | tf_op jit(solution)/shard_map/pallas_call | solution.py:540
  2.3 7.3 %all-to-all-start.4 = ((bf16[8,208,128]{2,1,0:T(8,128)(2,1)}), bf16[8,208,128]{2,1,0:T(8,128)(2,1)S(1)}, u32[]{:S(2)}, u32[]{:S(2)}) async-start(bf16[8,208,128]{2,1,0:T(8,128)(2,1)} %shard_map.102), calls=%async_computation.4 | async-start | bytes 851968 | tf_op jit(solution)/shard_map/all_to_all | solution.py:547
  9.6 6.7 %all_gather.3.tiles_ref = bf16[4,4,96,128]{3,2,1,0:T(8,128)(2,1)S(1)} all-gather(bf16[1,4,96,128]{3,2,1,0:T(8,128)(2,1)} %bitcast.271), channel_id=1, replica_groups=mesh['det'=4,'tm'=8] {'det'}, dimensions={0}, use_global_device_ids=true | all-gather | bytes 491520 | tf_op jit(solution)/shard_map/all_gather | solution.py:548
  16.3 5.7 %all-to-all-done.4.recv_ref = bf16[8,208,128]{2,1,0:T(8,128)(2,1)S(1)} async-done(((bf16[8,208,128]{2,1,0:T(8,128)(2,1)}), bf16[8,208,128]{2,1,0:T(8,128)(2,1)S(1)}, u32[]{:S(2)}, u32[]{:S(2)}) %all-to-all-start.4) | async-done | bytes 426016 | tf_op jit(solution)/shard_map/all_to_all | solution.py:547
  22.0 7.2 %shard_map.103 = (bf16[8,208,128]{2,1,0:T(8,128)(2,1)}, f32[8,192,128]{2,1,0:T(8,128)S(1)}, f32[192,8]{1,0:T(8,128)S(1)}, f32[24,128]{1,0:T(8,128)S(1)}) custom-call(bf16[8,208,128]{2,1,0:T(8,128)(2,1)S(1)} %all-to-all-done.4.recv_ref, bf16[4,4,96,128]{3,2,1,0:T(8,128)(2,1)S(1)} %all_gather.3.tiles_ref), custom_call_target="tpu_custom_call" | custom-call | tf_op jit(solution)/shard_map/pallas_call | solution.py:567
  29.2 3.6 %all-to-all-start.5 = ((bf16[8,208,128]{2,1,0:T(8,128)(2,1)}), bf16[8,208,128]{2,1,0:T(8,128)(2,1)S(1)}, u32[]{:S(2)}, u32[]{:S(2)}) async-start(bf16[8,208,128]{2,1,0:T(8,128)(2,1)} %get-tuple-element.140), calls=%async_computation.5 | async-start | bytes 851968 | tf_op jit(solution)/shard_map/all_to_all | solution.py:577
  32.8 0.1 slice.79
  32.9 0.1 pad_maximum_fusion.2
  33.0 0.6 reverse.1
  33.6 0.1 slice.161
  33.7 0.1 concatenate.21
  33.8 0.1 broadcast_in_dim.168.line_ref
  33.8 5.2 %shard_map.104.mat_ref = bf16[8,2176,256]{2,1,0:T(8,128)(2,1)S(1)} custom-call(f32[8,1,2304]{2,1,0:T(1,128)S(1)} %broadcast_in_dim.168.line_ref), custom_call_target="tpu_custom_call" | custom-call | tf_op jit(solution)/shard_map/pallas_call | solution.py:561
  39.0 3.4 %copy-done = bf16[8,2176,256]{2,1,0:T(8,128)(2,1)} copy-done((bf16[8,2176,256]{2,1,0:T(8,128)(2,1)}, bf16[8,2176,256]{2,1,0:T(8,128)(2,1)S(1)}, u32[]{:S(2)}) %copy-start) | copy-done | bytes 8912920
  42.4 2.2 %all-to-all-done.5.recv_ref = bf16[8,208,128]{2,1,0:T(8,128)(2,1)S(1)} async-done(((bf16[8,208,128]{2,1,0:T(8,128)(2,1)}), bf16[8,208,128]{2,1,0:T(8,128)(2,1)S(1)}, u32[]{:S(2)}, u32[]{:S(2)}) %all-to-all-start.5) | async-done | bytes 426016 | tf_op jit(solution)/shard_map/all_to_all | solution.py:577
  44.6 3.5 %copy-done.1 = bf16[8,2176,256]{2,1,0:T(8,128)(2,1)S(1)} copy-done((bf16[8,2176,256]{2,1,0:T(8,128)(2,1)S(1)}, bf16[8,2176,256]{2,1,0:T(8,128)(2,1)}, u32[]{:S(2)}) %copy-start.1) | copy-done | bytes 8912920
  48.2 9.5 %shard_map.105 = (f32[2,4,96,128]{3,2,1,0:T(8,128)S(1)}, bf16[2,4,96,128]{3,2,1,0:T(8,128)(2,1)S(1)}) custom-call(s32[1]{0:T(128)} %bitcast.74.core_ref, bf16[8,208,128]{2,1,0:T(8,128)(2,1)S(1)} %all-to-all-done.5.recv_ref, bf16[8,2176,256]{2,1,0:T(8,128)(2,1)S(1)} %copy-done.1, f32[8,192,128]{2,1,0:T(8,128)S(1)} %get-tuple-element.141.fields_ref, ...), custom_call_target="tpu_custom_call" | custom-call | tf_op jit(solution)/shard_map/pallas_call | solution.py:584
  57.8 0.1 collective-permute-start.2
  57.9 1.4 %collective-permute-done.2 = bf16[2,4,96,128]{3,2,1,0:T(8,128)(2,1)S(1)} collective-permute-done((bf16[2,4,96,128]{3,2,1,0:T(8,128)(2,1)S(1)}, bf16[2,4,96,128]{3,2,1,0:T(8,128)(2,1)S(1)}, u32[]{:S(2)}, u32[]{:S(2)}) %collective-permute-start.2) | collective-permute-done | bytes 196640 | tf_op jit(solution)/shard_map/ppermute | solution.py:600
  59.3 2.1 %collective-permute-start.3 = (bf16[4,96,128]{2,1,0:T(8,128)(2,1)S(1)}, bf16[4,96,128]{2,1,0:T(8,128)(2,1)S(1)}, u32[]{:S(2)}, u32[]{:S(2)}) collective-permute-start(bf16[4,96,128]{2,1,0:T(8,128)(2,1)S(1)} %fusion.68), channel_id=1, source_target_pairs={{0,16},{8,24},{16,0},{24,8},{1,17},{9,25},{17,1},{25,9},{2,18},{10... | collective-permute-start | bytes 294920 | tf_op jit(solution)/shard_map/ppermute | solution.py:609
  61.4 3.1 %collective-permute-done.3 = bf16[4,96,128]{2,1,0:T(8,128)(2,1)S(1)} collective-permute-done((bf16[4,96,128]{2,1,0:T(8,128)(2,1)S(1)}, bf16[4,96,128]{2,1,0:T(8,128)(2,1)S(1)}, u32[]{:S(2)}, u32[]{:S(2)}) %collective-permute-start.3) | collective-permute-done | bytes 98336 | tf_op jit(solution)/shard_map/ppermute | solution.py:609
  64.6 0.5 slice.106
  66.5 0.2 conditional.1
  66.7 0.7 copy-done.5
  (26 shorter events, 0.1 us)
Async XLA Ops:
  0.0 32.8 %copy-start.6 = (f32[8,1025]{1,0:T(8,128)S(1)}, f32[8,1025]{1,0:T(8,128)}, u32[]{:S(2)}) copy-start(f32[8,1025]{1,0:T(8,128)} %param.27) | copy-start | bytes 98404
  2.3 19.7 %all-to-all-start.4 = ((bf16[8,208,128]{2,1,0:T(8,128)(2,1)}), bf16[8,208,128]{2,1,0:T(8,128)(2,1)S(1)}, u32[]{:S(2)}, u32[]{:S(2)}) async-start(bf16[8,208,128]{2,1,0:T(8,128)(2,1)} %shard_map.102), calls=%async_computation.4 | async-start | bytes 851968 | tf_op jit(solution)/shard_map/all_to_all | solution.py:547
  29.2 15.5 %all-to-all-start.5 = ((bf16[8,208,128]{2,1,0:T(8,128)(2,1)}), bf16[8,208,128]{2,1,0:T(8,128)(2,1)S(1)}, u32[]{:S(2)}, u32[]{:S(2)}) async-start(bf16[8,208,128]{2,1,0:T(8,128)(2,1)} %get-tuple-element.140), calls=%async_computation.5 | async-start | bytes 851968 | tf_op jit(solution)/shard_map/all_to_all | solution.py:577
  39.0 3.4 %copy-start = (bf16[8,2176,256]{2,1,0:T(8,128)(2,1)}, bf16[8,2176,256]{2,1,0:T(8,128)(2,1)S(1)}, u32[]{:S(2)}) copy-start(bf16[8,2176,256]{2,1,0:T(8,128)(2,1)S(1)} %shard_map.104.mat_ref) | copy-start | bytes 26738692
  44.6 3.5 %copy-start.1 = (bf16[8,2176,256]{2,1,0:T(8,128)(2,1)S(1)}, bf16[8,2176,256]{2,1,0:T(8,128)(2,1)}, u32[]{:S(2)}) copy-start(bf16[8,2176,256]{2,1,0:T(8,128)(2,1)} %copy-done) | copy-start | bytes 26738692
  48.2 18.2 %copy-start.2 = (s32[8,2048]{1,0:T(8,128)S(1)}, s32[8,2048]{1,0:T(8,128)}, u32[]{:S(2)}) copy-start(s32[8,2048]{1,0:T(8,128)} %r_ref.1) | copy-start | bytes 196612
  48.2 18.2 %copy-start.3 = (s32[8,2048]{1,0:T(8,128)S(1)}, s32[8,2048]{1,0:T(8,128)}, u32[]{:S(2)}) copy-start(s32[8,2048]{1,0:T(8,128)} %c_ref.1) | copy-start | bytes 196612
  48.2 18.2 %copy-start.4 = (f32[8,2048]{1,0:T(8,128)S(1)}, f32[8,2048]{1,0:T(8,128)}, u32[]{:S(2)}) copy-start(f32[8,2048]{1,0:T(8,128)} %ang_ref.1) | copy-start | bytes 196612
  48.2 18.2 %copy-start.7 = (bf16[8,2048]{1,0:T(8,128)(2,1)S(1)}, bf16[8,2048]{1,0:T(8,128)(2,1)}, u32[]{:S(2)}) copy-start(bf16[8,2048]{1,0:T(8,128)(2,1)} %fr_ref.1) | copy-start | bytes 98308
  48.2 18.2 %copy-start.8 = (bf16[8,2048]{1,0:T(8,128)(2,1)S(1)}, bf16[8,2048]{1,0:T(8,128)(2,1)}, u32[]{:S(2)}) copy-start(bf16[8,2048]{1,0:T(8,128)(2,1)} %fc_ref.1) | copy-start | bytes 98308
  48.2 18.2 %copy-start.9 = (s32[8,16]{1,0:T(8,128)S(1)}, s32[8,16]{1,0:T(8,128)}, u32[]{:S(2)}) copy-start(s32[8,16]{1,0:T(8,128)} %slot_ref.1) | copy-start | bytes 1540
  48.2 18.2 %copy-start.10 = (s32[1,1,32]{2,1,0:T(1,128)S(1)}, s32[1,1,32]{2,1,0:T(1,128)}, u32[]{:S(2)}) copy-start(s32[1,1,32]{2,1,0:T(1,128)} %param.20) | copy-start | bytes 388
  48.2 18.2 %copy-start.11 = (s32[32]{0:T(128)S(1)}, s32[32]{0:T(128)}, u32[]{:S(2)}) copy-start(s32[32]{0:T(128)} %th_ref.1) | copy-start | bytes 388
  57.8 1.5 %collective-permute-start.2 = (bf16[2,4,96,128]{3,2,1,0:T(8,128)(2,1)S(1)}, bf16[2,4,96,128]{3,2,1,0:T(8,128)(2,1)S(1)}, u32[]{:S(2)}, u32[]{:S(2)}) collective-permute-start(bf16[2,4,96,128]{3,2,1,0:T(8,128)(2,1)S(1)} %get-tuple-element.145), channel_id=1, source_target_pairs={{0,8},{8,0},{16,24},{24,16},{1,9},{9,1},{17,25},{25,17},{2,10},{10... | collective-permute-start | bytes 589832 | tf_op jit(solution)/shard_map/ppermute | solution.py:600
  59.3 5.2 %collective-permute-start.3 = (bf16[4,96,128]{2,1,0:T(8,128)(2,1)S(1)}, bf16[4,96,128]{2,1,0:T(8,128)(2,1)S(1)}, u32[]{:S(2)}, u32[]{:S(2)}) collective-permute-start(bf16[4,96,128]{2,1,0:T(8,128)(2,1)S(1)} %fusion.68), channel_id=1, source_target_pairs={{0,16},{8,24},{16,0},{24,8},{1,17},{9,25},{17,1},{25,9},{2,18},{10... | collective-permute-start | bytes 294920 | tf_op jit(solution)/shard_map/ppermute | solution.py:609
  66.7 0.7 %copy-start.5 = (f32[4,3,32,128]{3,2,1,0:T(8,128)}, f32[4,3,32,128]{3,2,1,0:T(8,128)S(1)}, u32[]{:S(2)}) copy-start(f32[4,3,32,128]{3,2,1,0:T(8,128)S(1)} %get-tuple-element.467) | copy-start | bytes 589828

commit v3 on v2

--- a/solution.py
+++ b/solution.py
@@ -93,7 +93,7 @@
 GROUP = 4
 UNROLL = 4
 META = 16
-VMEM_LIMIT = 40 * 1024 * 1024
+VMEM_LIMIT = 24 * 1024 * 1024
 f32 = jnp.float32
 bf16 = jnp.bfloat16
 
@@ -118,7 +118,22 @@
     return jnp.where(mask, 1.0, 0.0).astype(bf16)
 
 
-def pack_kernel(owners, cap, tile_dev, pt_ref, th_ref, slot_ref, r_ref, c_ref, fr_ref, fc_ref, ang_ref, out_ref, meta_ref):
+def pack_kernel(
+    owners,
+    cap,
+    tile_dev,
+    pt_ref,
+    th_ref,
+    slot_ref,
+    r_ref,
+    c_ref,
+    fr_ref,
+    fc_ref,
+    ang_ref,
+    out_ref,
+    counts_ref,
+    meta_ref,
+):
     dets, blocks = slot_ref.shape
     runs = dets * blocks
     width = r_ref.shape[1] // blocks
@@ -170,6 +185,9 @@
         meta_ref[o, 0:8, 0:cap] = facts[:, o * cap : (o + 1) * cap]
         meta_ref[o, 8:16, 0:owners] = counts
     out_ref[:, len(fields) * cap :, :] = meta_ref[...].astype(bf16)
+    meta_ref[0] = jnp.zeros(meta_ref.shape[1:], f32)
+    meta_ref[0, 0:8, 0:owners] = counts
+    counts_ref[...] = meta_ref[0].astype(bf16)
 
 
 def weights_of(fields_ref, axis, run, shape):
@@ -195,12 +213,14 @@
 
 
 def project_kernel(
-    cap, kept, recv_ref, tiles_ref, out_ref, fields_ref, ids_ref, seg_ref, scratch_ref, sig_ref, lanes_ref
+    cap, kept, tile_dev, recv_ref, tiles_ref, out_ref, fields_ref, ids_ref, seg_ref, scratch_ref, sig_ref, lanes_ref
 ):
     owners = recv_ref.shape[0]
     slots = owners * cap
     width = recv_ref.shape[2]
-    groups_det, tile_dev, rows_dev, side = tiles_ref.shape
+    groups_det, tile_rows, side = tiles_ref.shape
+    tile_rows = tile_rows - META
+    rows_dev = tile_rows // tile_dev
     part = rows_dev // 3
     for s in range(owners):
         lanes_ref[:, s * cap : (s + 1) * cap] = recv_ref[s, 6 * cap : 6 * cap + META, :].astype(f32)[0:8, 0:cap]
@@ -219,12 +239,6 @@
     stop = jnp.minimum(start + padded, float(kept))
     seg_ref[0:8, :] = start
     seg_ref[8:16, :] = stop
-    at = 6 * cap + 8
-    counts = jnp.concatenate([recv_ref[s, at : at + 8, :].astype(f32)[0:1] for s in range(owners)], axis=0)
-    most = jnp.max(jnp.max(counts, axis=0, keepdims=True), axis=1, keepdims=True)
-    fullest = jnp.max(jnp.sum(counts, axis=0, keepdims=True), axis=1, keepdims=True)
-    over = jnp.logical_or(most > cap, fullest + tile_dev * (GROUP - 1) > kept)
-    seg_ref[16:24, :] = jnp.broadcast_to(jnp.where(over, 1.0, 0.0), (8, width))
     where_to = jnp.sum(jnp.where(tile_hot, prefix + start[:, 0:1], 0.0), axis=0, keepdims=True)
     where_to = jnp.where(tile1 > 0, where_to, -1.0).astype(jnp.int32)
     order = ones_where(iota((kept, slots), 0) == where_to)
@@ -237,6 +251,8 @@
     for q in range(-(-kept // width)):
         many = min(width, kept - q * width)
         scratch_ref[q * 8 : q * 8 + 8, 0:many] = id_lanes[:, q * width : q * width + many]
+    for d in range(groups_det):
+        scratch_ref[4 + d : 5 + d, :] = tiles_ref[d, tile_rows:, :].astype(f32)[0:1]
     ids_ref[...] = dot_nt(order, facts)
     sorted_fields = []
     for f in range(6):
@@ -254,7 +270,8 @@
 
     def one_group(group):
         tile = tile_of(group, ends)
-        rows = jnp.concatenate([tiles_ref[d, tile] for d in range(groups_det)], axis=0)
+        at_tile = pl.ds(pl.multiple_of(tile * rows_dev, rows_dev), rows_dev)
+        rows = jnp.concatenate([tiles_ref[d, at_tile, :] for d in range(groups_det)], axis=0)
         base = group * GROUP
         cols = [weights_of(fields_ref, 1, base + k, (side, width)) for k in range(GROUP)]
         partial_rows = dot_nn(rows, jnp.concatenate(cols, axis=1))
@@ -292,7 +309,6 @@
 
 def toeplitz_kernel(line_ref, out_ref):
     lines, rows, width = out_ref.shape
-    width = width // 2
     blocks = rows // width
 
     def one(d, carry):
@@ -300,15 +316,13 @@
             at = (blocks - 1 - m) * width
             piece = jnp.broadcast_to(line_ref[d, :, at : at + 2 * width], (width, 2 * width))
             block = pltpu.roll(piece, width, 1, stride=1, stride_axis=0)[:, :width]
-            high = block.astype(bf16)
-            out_ref[d, m * width : (m + 1) * width, :width] = high
-            out_ref[d, m * width : (m + 1) * width, width:] = (block - high.astype(f32)).astype(bf16)
+            out_ref[d, m * width : (m + 1) * width, :] = block.astype(bf16)
         return carry
 
     lax.fori_loop(0, lines, one, 0)
 
 
-def filter_lines(blocks_dev, kept, recv_ref, mat_ref, filt_ref, line_ref):
+def filter_lines(blocks_dev, kept, recv_ref, mat_ref, coef_ref, filt_ref, line_ref):
     owners, rows, width = recv_ref.shape
     lines, padded, _ = line_ref.shape
     count = owners * blocks_dev
@@ -344,20 +358,24 @@
         lax.fori_loop(0, owners // together, one, 0)
     for d in range(lines):
         spread = jnp.concatenate([line_ref[d, m : m + count, :].astype(bf16) for m in range(spans)], axis=1)
-        both = dot_nn(spread, mat_ref[d])
-        filt_ref[d] = both[:, :width] + both[:, width:]
+        weight = coef_ref[d : d + 1, 0:1] + 1.0
+        rest = weight - weight.astype(bf16).astype(f32)
+        filt_ref[d] = dot_nn(spread, mat_ref[d]) + rest * line_ref[d, edge : edge + count, :]
 
 
 def back_kernel(
     blocks_dev,
+    cap,
     core_ref,
     recv_ref,
     mat_ref,
+    coef_ref,
     fields_ref,
     ids_ref,
     seg_ref,
     mine_ref,
     theirs_ref,
+    over_ref,
     filt_ref,
     line_ref,
     scaled_ref,
@@ -365,11 +383,18 @@
 ):
     width = fields_ref.shape[2]
     kept = fields_ref.shape[1]
-    filter_lines(blocks_dev, kept, recv_ref, mat_ref, filt_ref, line_ref)
+    filter_lines(blocks_dev, kept, recv_ref, mat_ref, coef_ref, filt_ref, line_ref)
     pairs, tile_dev, rows_dev, side = mine_ref.shape
     part = rows_dev // 3
     core = core_ref[0]
-    poison = jnp.where(seg_ref[16:17, :] > 0.5, jnp.nan, 0.0)
+    owners = recv_ref.shape[0]
+    most = totals = jnp.zeros((4, width), f32)
+    for s in range(owners):
+        counts = recv_ref[s, kept : kept + META, :].astype(f32)[4:8]
+        most, totals = jnp.maximum(most, counts), totals + counts
+    most = jnp.max(most)
+    fullest = jnp.max(totals) + tile_dev * (GROUP - 1)
+    over_ref[0] = jnp.logical_or(most > cap, fullest > kept).astype(jnp.int32)
     lines, count, _ = filt_ref.shape
     ids = ids_ref[...]
     at = ids[:, 2:3] * count + ids[:, 3:4] * blocks_dev + ids[:, 1:2]
@@ -409,8 +434,8 @@
                 base = p * side + h * 2 * part
                 mine = acc_ref[tile, pl.ds(pl.multiple_of(base + core * part, part), part), :]
                 theirs = acc_ref[tile, pl.ds(pl.multiple_of(base + (1 - core) * part, part), part), :]
-                mine_ref[h, tile, p * part : (p + 1) * part, :] = mine + poison
-                theirs_ref[h, tile, p * part : (p + 1) * part, :] = (theirs + poison).astype(bf16)
+                mine_ref[h, tile, p * part : (p + 1) * part, :] = mine
+                theirs_ref[h, tile, p * part : (p + 1) * part, :] = theirs.astype(bf16)
 
 
 def call(kernel, out, scratch=(), **more):
@@ -537,15 +562,28 @@
     smem = pl.BlockSpec(memory_space=pltpu.SMEM)
     vmem = pl.BlockSpec(memory_space=pltpu.VMEM)
 
-    packed = call(
+    packed, counts = call(
         functools.partial(pack_kernel, owners, cap, tile_dev),
-        jax.ShapeDtypeStruct((owners, 6 * cap + META, width), bf16),
+        (
+            jax.ShapeDtypeStruct((owners, 6 * cap + META, width), bf16),
+            jax.ShapeDtypeStruct((META, width), bf16),
+        ),
         [pltpu.VMEM((owners, META, width), f32)],
         in_specs=[smem, smem] + [vmem] * 6,
-        out_specs=vmem,
-    )(piece_list, tile_home, run_slot, hit_row, hit_col, frac_row, frac_col, angle)
+        out_specs=(vmem, vmem),
+    )(
+        piece_list,
+        tile_home,
+        run_slot,
+        hit_row,
+        hit_col,
+        frac_row,
+        frac_col,
+        angle,
+    )
     recv = lax.all_to_all(packed, "tm", split_axis=0, concat_axis=0, tiled=True)
-    tiles = lax.all_gather(sky_map.reshape(tile_dev, 3 * part, side), "det", axis=0)
+    rows = jnp.concatenate([sky_map.reshape(tile_dev * 3 * part, side), counts], axis=0)
+    tiles = lax.all_gather(rows, "det", axis=0)
 
     weights = jnp.concatenate([noise_coef[:, :1] + 1.0, noise_coef[:, 1:]], axis=1)
     line = jnp.concatenate(
@@ -560,17 +598,17 @@
     spans = 2 * (half_band // width) + 1
     matrix = call(
         toeplitz_kernel,
-        pltpu.VMEM((dets, spans * width, 2 * width), bf16),
+        pltpu.VMEM((dets, spans * width, width), bf16),
     )(line[:, None, :])
 
     notes = round_up(kept, width) // width * 8
     sent, fields, ids, seg = call(
-        functools.partial(project_kernel, cap, kept),
+        functools.partial(project_kernel, cap, kept, tile_dev),
         (
             jax.ShapeDtypeStruct((owners, kept + notes, width), bf16),
             jax.ShapeDtypeStruct((8, kept, width), f32),
             jax.ShapeDtypeStruct((kept, 8), f32),
-            jax.ShapeDtypeStruct((24, width), f32),
+            jax.ShapeDtypeStruct((16, width), f32),
         ),
         [pltpu.VMEM((notes, width), f32), pltpu.VMEM((kept, width), f32), pltpu.VMEM((8, slots), f32)],
     )(recv, tiles)
@@ -581,11 +619,12 @@
     core = lax.rem(place, 2)
     half = lax.div(place, 2)
     pairs = groups_det // 2
-    mine, theirs = call(
-        functools.partial(back_kernel, blocks),
+    mine, theirs, over = call(
+        functools.partial(back_kernel, blocks, cap),
         (
             jax.ShapeDtypeStruct((pairs, tile_dev, 3 * part, side), f32),
             jax.ShapeDtypeStruct((pairs, tile_dev, 3 * part, side), bf16),
+            jax.ShapeDtypeStruct((1,), jnp.int32),
         ),
         [
             pltpu.VMEM((dets, count, width), f32),
@@ -593,9 +632,9 @@
             pltpu.VMEM((3, kept, width), f32),
             pltpu.VMEM((tile_dev, 3 * side, side), f32),
         ],
-        in_specs=[smem] + [vmem] * 5,
-        out_specs=(vmem, vmem),
-    )(core[None].astype(jnp.int32), heard, matrix, fields, ids, seg)
+        in_specs=[smem] + [vmem] * 6,
+        out_specs=(vmem, vmem, smem),
+    )(core[None].astype(jnp.int32), heard, matrix, noise_coef, fields, ids, seg)
 
     beside = lax.ppermute(theirs, "det", [(i, i ^ 1) for i in range(groups_det)])
 
@@ -603,22 +642,26 @@
         pick = lambda values: lax.dynamic_index_in_dim(values, h, 0, keepdims=False).astype(f32)
         return pick(mine) + pick(beside)
 
-    total = of_pair(half)
+    others = []
     for step in range(1, pairs):
         ring = [(i, (i + 2 * step) % groups_det) for i in range(groups_det)]
-        total = total + lax.ppermute(
-            of_pair(lax.rem(half + step, pairs)).astype(bf16), "det", ring
-        ).astype(f32)
-    total = total.reshape(tile_dev, 3, part, side)
+        sent_on = of_pair(lax.rem(half + step, pairs)).astype(bf16)
+        others.append(lax.ppermute(sent_on, "det", ring))
+
+    def summed(_):
+        total = of_pair(half)
+        for other in others:
+            total = total + other.astype(f32)
+        return total.reshape(tile_dev, 3, part, side)
 
     def travelling(_):
         position = positions_of(piece_list, tile_home)
+        whole = tiles[:, : tile_dev * 3 * part].reshape(groups_det, tile_dev, 3 * part, side)
         return whole_tiles(
-            tiles, position, run_slot, hit_row, hit_col, frac_row, frac_col, angle, noise_coef
+            whole, position, run_slot, hit_row, hit_col, frac_row, frac_col, angle, noise_coef
         )
 
-    fits = jnp.logical_not(jnp.isnan(total[0, 0, 0, 0]))
-    return lax.cond(fits, lambda t: t, travelling, total)
+    return lax.cond(over[0] == 0, summed, travelling, 0)
 
 
 def solution(mesh):

time: 67.6 us -> 65.5 us (0.969)
  local copies, waits for them, and re-layouts: 9.11 us -> 5.93 us
  Pallas kernels: 24.2 us -> 22.3 us
  waiting for transfers between devices: 12.4 us -> 14 us
  starting transfers between devices: 13.1 us -> 14.4 us
  other arithmetic: 0.13 us -> 1.04 us
  between operations: 1.51 us -> 0.83 us
    all_to_all x1, waiting for transfers between devices: 2.21 us -> 5.22 us  [body(): heard = lax.all_to_all(sent, 'tm', split_axis=0, concat_axis=0, tiled=True)]
    unnamed x26, local copies, waits for them, and re-layouts: 8.37 us -> 5.72 us
    pallas_call x4, Pallas kernels: 24.2 us -> 22.3 us  [the longest x1 10 us: body(): call(functools.partial(back_kernel, blocks, cap), (jax.ShapeDtypeStruct((...]
    concatenate x0 -> x1, other arithmetic: none -> 0.9 us  [body(): jnp.concatenate([sky_map.reshape(tile_dev * 3 * part, side), counts], axi...]
    all_to_all x1, waiting for transfers between devices: 5.72 us -> 4.95 us  [body(): recv = lax.all_to_all(packed, 'tm', split_axis=0, concat_axis=0, tiled=True)]
  transfers between devices with their start and end apart: 4 -> 4, of which waited for: 4 -> 4; matrix products, arithmetic and copies ran while one was open for 1% -> 3% of each run, Pallas kernels for 8% -> 4%
where the time goes in v3:
time: 65.5 us; the launch traced here: 65.3 us
  Pallas kernels  22.3 us (34%)
  starting transfers between devices  14.4 us (22%)
  waiting for transfers between devices  14 us (21%)
  blocking collectives  6.52 us (10%)
  local copies, waits for them, and re-layouts  5.93 us (9%)
  other arithmetic  1.04 us (2%)
  between operations  0.83 us (1%)
    pallas_call x1, Pallas kernels, body(): call(functools.partial(back_kernel, blocks, cap), (jax.ShapeDtypeStruct((...  10 us
    all_to_all x1, starting transfers between devices, body(): recv = lax.all_to_all(packed, 'tm', split_axis=0, concat_axis=0, tiled=True)  7.29 us
    pallas_call x1, Pallas kernels, body(): call(functools.partial(project_kernel, cap, kept, tile_dev), (jax.ShapeDt...  7.11 us
    all_gather x1, blocking collectives, body(): tiles = lax.all_gather(rows, 'det', axis=0)  6.52 us
    unnamed x26, local copies, waits for them, and re-layouts  5.72 us
    all_to_all x1, waiting for transfers between devices, body(): heard = lax.all_to_all(sent, 'tm', split_axis=0, concat_axis=0, tiled=True)  5.22 us
    all_to_all x1, waiting for transfers between devices, body(): recv = lax.all_to_all(packed, 'tm', split_axis=0, concat_axis=0, tiled=True)  4.95 us
    all_to_all x1, starting transfers between devices, body(): heard = lax.all_to_all(sent, 'tm', split_axis=0, concat_axis=0, tiled=True)  4.24 us
  transfers between devices with their start and end apart: 4, of which 4 were waited for; matrix products, arithmetic and copies ran while one was open for 3% of the time, Pallas kernels for 4%

profile of v3, /device:TPU:0, one launch (start us, length us, event | category | flops | bytes accessed | tf_op | source)
XLA Modules:
  0.0 65.3 jit_solution(10161506140371719433)
XLA Ops:
  0.0 2.3 %shard_map.102 = (bf16[8,208,128]{2,1,0:T(8,128)(2,1)}, bf16[16,128]{1,0:T(8,128)(2,1)S(1)}) custom-call(s32[32]{0:T(128)} %bitcast.274, s32[32]{0:T(128)} %th_ref.1, s32[8,16]{1,0:T(8,128)} %slot_ref.1, s32[8,2048]{1,0:T(8,128)} %r_ref.1, s32[8,2048]{1,0:T(8,128)} %c_ref.1, bf16[8,2048]{1,0:T(8,128)(2,1)} %fr_ref.1, bf16[8,2048]{1,0:T(8,128)(2,1)} %fc_ref.1, ...), custom_call_target="tpu_custom_call" | custom-call | tf_op jit(solution)/shard_map/pallas_call | solution.py:565
  2.3 7.3 %all-to-all-start.4 = ((bf16[8,208,128]{2,1,0:T(8,128)(2,1)}), bf16[8,208,128]{2,1,0:T(8,128)(2,1)S(1)}, u32[]{:S(2)}, u32[]{:S(2)}) async-start(bf16[8,208,128]{2,1,0:T(8,128)(2,1)} %get-tuple-element.154), calls=%async_computation.4 | async-start | bytes 851968 | tf_op jit(solution)/shard_map/all_to_all | solution.py:584
  9.6 0.9 %pad_maximum_fusion.2 = bf16[400,128]{1,0:T(8,128)(2,1)S(1)} fusion(bf16[16,128]{1,0:T(8,128)(2,1)S(1)} %get-tuple-element.155, bf16[384,128]{1,0:T(8,128)(2,1)} %bitcast.273), kind=kLoop, calls=%fused_computation.162 | loop fusion | flops 204800 | bytes 204800 | tf_op jit(solution)/shard_map/concatenate | solution.py:585
  10.5 6.5 %all-gather = bf16[1600,128]{1,0:T(8,128)(2,1)S(1)} all-gather(bf16[400,128]{1,0:T(8,128)(2,1)S(1)} %pad_maximum_fusion.2), channel_id=2, replica_groups=mesh['det'=4,'tm'=8] {'det'}, dimensions={0}, use_global_device_ids=true | all-gather | bytes 512000 | tf_op jit(solution)/shard_map/all_gather | solution.py:586
  17.0 5.0 %all-to-all-done.4.recv_ref = bf16[8,208,128]{2,1,0:T(8,128)(2,1)S(1)} async-done(((bf16[8,208,128]{2,1,0:T(8,128)(2,1)}), bf16[8,208,128]{2,1,0:T(8,128)(2,1)S(1)}, u32[]{:S(2)}, u32[]{:S(2)}) %all-to-all-start.4) | async-done | bytes 426016 | tf_op jit(solution)/shard_map/all_to_all | solution.py:584
  22.0 7.1 %shard_map.103 = (bf16[8,208,128]{2,1,0:T(8,128)(2,1)}, f32[8,192,128]{2,1,0:T(8,128)S(1)}, f32[192,8]{1,0:T(8,128)S(1)}, f32[16,128]{1,0:T(8,128)S(1)}) custom-call(bf16[8,208,128]{2,1,0:T(8,128)(2,1)S(1)} %all-to-all-done.4.recv_ref, bf16[4,400,128]{2,1,0:T(8,128)(2,1)S(1)} %bitcast.259), custom_call_target="tpu_custom_call" | custom-call | tf_op jit(solution)/shard_map/pallas_call | solution.py:605
  29.1 4.2 %all-to-all-start.5 = ((bf16[8,208,128]{2,1,0:T(8,128)(2,1)}), bf16[8,208,128]{2,1,0:T(8,128)(2,1)S(1)}, u32[]{:S(2)}, u32[]{:S(2)}) async-start(bf16[8,208,128]{2,1,0:T(8,128)(2,1)} %get-tuple-element.156), calls=%async_computation.5 | async-start | bytes 851968 | tf_op jit(solution)/shard_map/all_to_all | solution.py:615
  33.3 0.1 slice.79
  33.4 0.1 pad_maximum_fusion.3
  33.5 0.6 reverse.1
  34.1 0.1 slice.159
  34.2 0.1 concatenate.25
  34.3 0.1 broadcast_in_dim.168.line_ref
  34.4 2.9 %shard_map.104.mat_ref = bf16[8,2176,128]{2,1,0:T(8,128)(2,1)S(1)} custom-call(f32[8,1,2304]{2,1,0:T(1,128)S(1)} %broadcast_in_dim.168.line_ref), custom_call_target="tpu_custom_call" | custom-call | tf_op jit(solution)/shard_map/pallas_call | solution.py:599
  37.3 2.0 %copy-done = bf16[8,2176,128]{2,1,0:T(8,128)(2,1)} copy-done((bf16[8,2176,128]{2,1,0:T(8,128)(2,1)}, bf16[8,2176,128]{2,1,0:T(8,128)(2,1)S(1)}, u32[]{:S(2)}) %copy-start) | copy-done | bytes 4456472
  39.3 5.2 %all-to-all-done.5.recv_ref = bf16[8,208,128]{2,1,0:T(8,128)(2,1)S(1)} async-done(((bf16[8,208,128]{2,1,0:T(8,128)(2,1)}), bf16[8,208,128]{2,1,0:T(8,128)(2,1)S(1)}, u32[]{:S(2)}, u32[]{:S(2)}) %all-to-all-start.5) | async-done | bytes 426016 | tf_op jit(solution)/shard_map/all_to_all | solution.py:615
  44.5 2.3 %copy-done.1 = bf16[8,2176,128]{2,1,0:T(8,128)(2,1)S(1)} copy-done((bf16[8,2176,128]{2,1,0:T(8,128)(2,1)S(1)}, bf16[8,2176,128]{2,1,0:T(8,128)(2,1)}, u32[]{:S(2)}) %copy-start.1) | copy-done | bytes 4456472
  46.8 10.0 %shard_map.105 = (f32[2,4,96,128]{3,2,1,0:T(8,128)S(1)}, bf16[2,4,96,128]{3,2,1,0:T(8,128)(2,1)S(1)}, s32[1]{0:T(128)}) custom-call(s32[1]{0:T(128)} %bitcast.76.core_ref, bf16[8,208,128]{2,1,0:T(8,128)(2,1)S(1)} %all-to-all-done.5.recv_ref, bf16[8,2176,128]{2,1,0:T(8,128)(2,1)S(1)} %copy-done.1, f32[8,1025]{1,0:T(8,128)S(1)} %copy-done.2, ...), custom_call_target="tpu_custom_call" | custom-call | tf_op jit(solution)/shard_map/pallas_call | solution.py:622
  56.8 0.1 collective-permute-start.2
  56.9 1.4 %collective-permute-done.2 = bf16[2,4,96,128]{3,2,1,0:T(8,128)(2,1)S(1)} collective-permute-done((bf16[2,4,96,128]{3,2,1,0:T(8,128)(2,1)S(1)}, bf16[2,4,96,128]{3,2,1,0:T(8,128)(2,1)S(1)}, u32[]{:S(2)}, u32[]{:S(2)}) %collective-permute-start.2) | collective-permute-done | bytes 196640 | tf_op jit(solution)/shard_map/ppermute | solution.py:639
  58.4 2.8 %collective-permute-start.3 = (bf16[4,96,128]{2,1,0:T(8,128)(2,1)S(1)}, bf16[4,96,128]{2,1,0:T(8,128)(2,1)S(1)}, u32[]{:S(2)}, u32[]{:S(2)}) collective-permute-start(bf16[4,96,128]{2,1,0:T(8,128)(2,1)S(1)} %fusion.68), channel_id=1, source_target_pairs={{0,16},{8,24},{16,0},{24,8},{1,17},{9,25},{17,1},{25,9},{2,18},{10... | collective-permute-start | bytes 294920 | tf_op jit(solution)/shard_map/ppermute | solution.py:649
  61.8 2.5 %collective-permute-done.3 = bf16[4,96,128]{2,1,0:T(8,128)(2,1)S(1)} collective-permute-done((bf16[4,96,128]{2,1,0:T(8,128)(2,1)S(1)}, bf16[4,96,128]{2,1,0:T(8,128)(2,1)S(1)}, u32[]{:S(2)}, u32[]{:S(2)}) %collective-permute-start.3) | collective-permute-done | bytes 98336 | tf_op jit(solution)/shard_map/ppermute | solution.py:649
  64.3 0.3 conditional.1
  64.6 0.7 %copy-done.6 = f32[4,3,32,128]{3,2,1,0:T(8,128)} copy-done((f32[4,3,32,128]{3,2,1,0:T(8,128)}, f32[4,3,32,128]{3,2,1,0:T(8,128)S(1)}, u32[]{:S(2)}) %copy-start.6) | copy-done | bytes 196632
  (26 shorter events, 0.1 us)
Async XLA Ops:
  0.0 33.3 %copy-start.2 = (f32[8,1025]{1,0:T(8,128)S(1)}, f32[8,1025]{1,0:T(8,128)}, u32[]{:S(2)}) copy-start(f32[8,1025]{1,0:T(8,128)} %coef_ref.1) | copy-start | bytes 98404
  2.3 19.7 %all-to-all-start.4 = ((bf16[8,208,128]{2,1,0:T(8,128)(2,1)}), bf16[8,208,128]{2,1,0:T(8,128)(2,1)S(1)}, u32[]{:S(2)}, u32[]{:S(2)}) async-start(bf16[8,208,128]{2,1,0:T(8,128)(2,1)} %get-tuple-element.154), calls=%async_computation.4 | async-start | bytes 851968 | tf_op jit(solution)/shard_map/all_to_all | solution.py:584
  29.1 15.4 %all-to-all-start.5 = ((bf16[8,208,128]{2,1,0:T(8,128)(2,1)}), bf16[8,208,128]{2,1,0:T(8,128)(2,1)S(1)}, u32[]{:S(2)}, u32[]{:S(2)}) async-start(bf16[8,208,128]{2,1,0:T(8,128)(2,1)} %get-tuple-element.156), calls=%async_computation.5 | async-start | bytes 851968 | tf_op jit(solution)/shard_map/all_to_all | solution.py:615
  37.2 2.0 %copy-start = (bf16[8,2176,128]{2,1,0:T(8,128)(2,1)}, bf16[8,2176,128]{2,1,0:T(8,128)(2,1)S(1)}, u32[]{:S(2)}) copy-start(bf16[8,2176,128]{2,1,0:T(8,128)(2,1)S(1)} %shard_map.104.mat_ref) | copy-start | bytes 13369348
  44.5 2.3 %copy-start.1 = (bf16[8,2176,128]{2,1,0:T(8,128)(2,1)S(1)}, bf16[8,2176,128]{2,1,0:T(8,128)(2,1)}, u32[]{:S(2)}) copy-start(bf16[8,2176,128]{2,1,0:T(8,128)(2,1)} %copy-done) | copy-start | bytes 13369348
  46.8 17.5 %copy-start.3 = (s32[8,2048]{1,0:T(8,128)S(1)}, s32[8,2048]{1,0:T(8,128)}, u32[]{:S(2)}) copy-start(s32[8,2048]{1,0:T(8,128)} %r_ref.1) | copy-start | bytes 196612
  46.8 17.5 %copy-start.4 = (s32[8,2048]{1,0:T(8,128)S(1)}, s32[8,2048]{1,0:T(8,128)}, u32[]{:S(2)}) copy-start(s32[8,2048]{1,0:T(8,128)} %c_ref.1) | copy-start | bytes 196612
  46.8 17.5 %copy-start.5 = (f32[8,2048]{1,0:T(8,128)S(1)}, f32[8,2048]{1,0:T(8,128)}, u32[]{:S(2)}) copy-start(f32[8,2048]{1,0:T(8,128)} %ang_ref.1) | copy-start | bytes 196612
  46.8 17.5 %copy-start.7 = (bf16[8,2048]{1,0:T(8,128)(2,1)S(1)}, bf16[8,2048]{1,0:T(8,128)(2,1)}, u32[]{:S(2)}) copy-start(bf16[8,2048]{1,0:T(8,128)(2,1)} %fr_ref.1) | copy-start | bytes 98308
  46.8 17.5 %copy-start.8 = (bf16[8,2048]{1,0:T(8,128)(2,1)S(1)}, bf16[8,2048]{1,0:T(8,128)(2,1)}, u32[]{:S(2)}) copy-start(bf16[8,2048]{1,0:T(8,128)(2,1)} %fc_ref.1) | copy-start | bytes 98308
  46.8 17.5 %copy-start.9 = (s32[8,16]{1,0:T(8,128)S(1)}, s32[8,16]{1,0:T(8,128)}, u32[]{:S(2)}) copy-start(s32[8,16]{1,0:T(8,128)} %slot_ref.1) | copy-start | bytes 1540
  46.8 17.5 %copy-start.10 = (s32[1,1,32]{2,1,0:T(1,128)S(1)}, s32[1,1,32]{2,1,0:T(1,128)}, u32[]{:S(2)}) copy-start(s32[1,1,32]{2,1,0:T(1,128)} %param.20) | copy-start | bytes 388
  46.8 17.5 %copy-start.11 = (s32[32]{0:T(128)S(1)}, s32[32]{0:T(128)}, u32[]{:S(2)}) copy-start(s32[32]{0:T(128)} %th_ref.1) | copy-start | bytes 388
  56.8 1.5 %collective-permute-start.2 = (bf16[2,4,96,128]{3,2,1,0:T(8,128)(2,1)S(1)}, bf16[2,4,96,128]{3,2,1,0:T(8,128)(2,1)S(1)}, u32[]{:S(2)}, u32[]{:S(2)}) collective-permute-start(bf16[2,4,96,128]{3,2,1,0:T(8,128)(2,1)S(1)} %get-tuple-element.162), channel_id=1, source_target_pairs={{0,8},{8,0},{16,24},{24,16},{1,9},{9,1},{17,25},{25,17},{2,10},{10... | collective-permute-start | bytes 589832 | tf_op jit(solution)/shard_map/ppermute | solution.py:639
  58.4 5.9 %collective-permute-start.3 = (bf16[4,96,128]{2,1,0:T(8,128)(2,1)S(1)}, bf16[4,96,128]{2,1,0:T(8,128)(2,1)S(1)}, u32[]{:S(2)}, u32[]{:S(2)}) collective-permute-start(bf16[4,96,128]{2,1,0:T(8,128)(2,1)S(1)} %fusion.68), channel_id=1, source_target_pairs={{0,16},{8,24},{16,0},{24,8},{1,17},{9,25},{17,1},{25,9},{2,18},{10... | collective-permute-start | bytes 294920 | tf_op jit(solution)/shard_map/ppermute | solution.py:649
  64.6 0.7 %copy-start.6 = (f32[4,3,32,128]{3,2,1,0:T(8,128)}, f32[4,3,32,128]{3,2,1,0:T(8,128)S(1)}, u32[]{:S(2)}) copy-start(f32[4,3,32,128]{3,2,1,0:T(8,128)S(1)} %get-tuple-element.484) | copy-start | bytes 589828

commit v4 on v3

--- a/solution.py
+++ b/solution.py
@@ -91,7 +91,7 @@
 
 
 GROUP = 4
-UNROLL = 4
+UNROLL = 6
 META = 16
 VMEM_LIMIT = 24 * 1024 * 1024
 f32 = jnp.float32
@@ -190,9 +190,9 @@
     counts_ref[...] = meta_ref[0].astype(bf16)
 
 
-def weights_of(fields_ref, axis, run, shape):
+def weights_of(fields_ref, axis, index, run, shape):
     index, high, low = (
-        fields_ref[f + axis, pl.ds(run, 1), :].astype(bf16) for f in (0, 2, 6)
+        fields_ref[f, pl.ds(run, 1), :].astype(bf16) for f in (index, 2 + axis, 6 + axis)
     )
     rows = iota(shape, 0).astype(f32).astype(bf16)
     zero = jnp.zeros((), bf16)
@@ -213,7 +213,19 @@
 
 
 def project_kernel(
-    cap, kept, tile_dev, recv_ref, tiles_ref, out_ref, fields_ref, ids_ref, seg_ref, scratch_ref, sig_ref, lanes_ref
+    cap,
+    kept,
+    tile_dev,
+    recv_ref,
+    tiles_ref,
+    out_ref,
+    fields_ref,
+    ids_ref,
+    seg_ref,
+    scratch_ref,
+    sig_ref,
+    lanes_ref,
+    half_ref,
 ):
     owners = recv_ref.shape[0]
     slots = owners * cap
@@ -259,33 +271,38 @@
         field = jnp.concatenate([recv_ref[s, f * cap : (f + 1) * cap, :] for s in range(owners)], axis=0)
         sorted_fields.append(dot_nn(order, field))
     twice = 2.0 * (sorted_fields[4] + sorted_fields[5])
-    for f in range(4):
+    reach = side // 2 + META
+    upper = jnp.where(sorted_fields[0] >= side // 2, 1.0, 0.0)
+    fields_ref[0] = sorted_fields[0] - upper * (side - reach)
+    fields_ref[1] = sorted_fields[1] + upper * side
+    for f in (2, 3):
         fields_ref[f] = sorted_fields[f]
+    fields_ref[8] = sorted_fields[0]
+    fields_ref[9] = sorted_fields[1]
     fields_ref[4] = jnp.cos(twice)
     fields_ref[5] = jnp.sin(twice)
     fields_ref[6] = (1.0 - sorted_fields[2]).astype(bf16).astype(f32)
     fields_ref[7] = (1.0 - sorted_fields[3]).astype(bf16).astype(f32)
     sig_ref[...] = jnp.zeros_like(sig_ref)
+    for tile in range(tile_dev):
+        for p in range(3):
+            at = tile * rows_dev + p * part
+            plane = jnp.concatenate([tiles_ref[d, at : at + part, :] for d in range(groups_det)], axis=0)
+            halves = jnp.concatenate([plane[:reach], plane[side - reach :]], axis=1)
+            half_ref[tile, p * reach : (p + 1) * reach, :] = halves
     ends = segments(seg_ref, tile_dev)
 
     def one_group(group):
         tile = tile_of(group, ends)
-        at_tile = pl.ds(pl.multiple_of(tile * rows_dev, rows_dev), rows_dev)
-        rows = jnp.concatenate([tiles_ref[d, at_tile, :] for d in range(groups_det)], axis=0)
         base = group * GROUP
-        cols = [weights_of(fields_ref, 1, base + k, (side, width)) for k in range(GROUP)]
-        partial_rows = dot_nn(rows, jnp.concatenate(cols, axis=1))
+        cols = [weights_of(fields_ref, 1, 1, base + k, (2 * side, width)) for k in range(GROUP)]
+        partial_rows = dot_nn(half_ref[tile], jnp.concatenate(cols, axis=1))
         for k in range(GROUP):
-            row_weight = weights_of(fields_ref, 0, base + k, (side, width)).astype(f32)
+            row_weight = weights_of(fields_ref, 0, 0, base + k, (reach, width)).astype(f32)
             values = []
             for p in range(3):
-                total = None
-                for d in range(groups_det):
-                    at = d * rows_dev + p * part
-                    term = partial_rows[at : at + part, k * width : (k + 1) * width]
-                    term = term * row_weight[d * part : (d + 1) * part]
-                    total = term if total is None else total + term
-                values.append(jnp.sum(total, axis=0, keepdims=True))
+                term = partial_rows[p * reach : (p + 1) * reach, k * width : (k + 1) * width]
+                values.append(jnp.sum(term * row_weight, axis=0, keepdims=True))
             cos = fields_ref[4, pl.ds(base + k, 1), :]
             sin = fields_ref[5, pl.ds(base + k, 1), :]
             sig_ref[pl.ds(base + k, 1), :] = values[0] + cos * values[1] + sin * values[2]
@@ -416,8 +433,8 @@
         base = group * GROUP
         cols, terms = [], []
         for k in range(GROUP):
-            cols.append(weights_of(fields_ref, 1, base + k, (side, width)))
-            row_weight = weights_of(fields_ref, 0, base + k, (side, width)).astype(f32)
+            cols.append(weights_of(fields_ref, 1, 9, base + k, (side, width)))
+            row_weight = weights_of(fields_ref, 0, 8, base + k, (side, width)).astype(f32)
             scaled = [scaled_ref[p, pl.ds(base + k, 1), :] for p in range(3)]
             terms.append(jnp.concatenate([(x * row_weight).astype(bf16) for x in scaled], axis=0))
         return dot_nt(jnp.concatenate(terms, axis=1), jnp.concatenate(cols, axis=1))
@@ -556,8 +573,9 @@
     listed = piece_tiles.shape[2]
     half_band = noise_coef.shape[1] - 1
     cap = round_up(2 * runs // min(owners, listed), META)
-    kept = round_up(runs + runs // 2, META)
+    kept = round_up(runs + runs // 2, math.lcm(META, GROUP * UNROLL))
     slots = owners * cap
+    reach = side // 2 + META
     piece_list = piece_tiles.reshape(listed)
     smem = pl.BlockSpec(memory_space=pltpu.SMEM)
     vmem = pl.BlockSpec(memory_space=pltpu.VMEM)
@@ -606,11 +624,16 @@
         functools.partial(project_kernel, cap, kept, tile_dev),
         (
             jax.ShapeDtypeStruct((owners, kept + notes, width), bf16),
-            jax.ShapeDtypeStruct((8, kept, width), f32),
+            jax.ShapeDtypeStruct((10, kept, width), f32),
             jax.ShapeDtypeStruct((kept, 8), f32),
             jax.ShapeDtypeStruct((16, width), f32),
         ),
-        [pltpu.VMEM((notes, width), f32), pltpu.VMEM((kept, width), f32), pltpu.VMEM((8, slots), f32)],
+        [
+            pltpu.VMEM((notes, width), f32),
+            pltpu.VMEM((kept, width), f32),
+            pltpu.VMEM((8, slots), f32),
+            pltpu.VMEM((tile_dev, 3 * reach, 2 * side), bf16),
+        ],
     )(recv, tiles)
     heard = lax.all_to_all(sent, "tm", split_axis=0, concat_axis=0, tiled=True)
 

time: 65.5 us -> 65 us (level)
  starting transfers between devices: 14.4 us -> 11.5 us
  waiting for transfers between devices: 14 us -> 15.8 us
    ppermute x1, starting transfers between devices: 2.79 us -> 0.67 us  [body(): others.append(lax.ppermute(sent_on, 'det', ring))]
    ppermute x1, waiting for transfers between devices: 2.46 us -> 3.59 us  [body(): others.append(lax.ppermute(sent_on, 'det', ring))]
    all_to_all x1, starting transfers between devices: 4.24 us -> 3.46 us  [body(): heard = lax.all_to_all(sent, 'tm', split_axis=0, concat_axis=0, tiled=True)]
where the time goes in v4:
time: 65 us; the launch traced here: 64.7 us
  Pallas kernels  22.8 us (35%)
  waiting for transfers between devices  15.8 us (24%)
  starting transfers between devices  11.5 us (18%)
  blocking collectives  6.52 us (10%)
  local copies, waits for them, and re-layouts  5.93 us (9%)
  other arithmetic  1.04 us (2%)
  between operations  0.84 us (1%)
    pallas_call x1, Pallas kernels, body(): call(functools.partial(back_kernel, blocks, cap), (jax.ShapeDtypeStruct((...  10.5 us
    all_to_all x1, starting transfers between devices, body(): recv = lax.all_to_all(packed, 'tm', split_axis=0, concat_axis=0, tiled=True)  7.29 us
    pallas_call x1, Pallas kernels, body(): call(functools.partial(project_kernel, cap, kept, tile_dev), (jax.ShapeDt...  7.12 us
    all_gather x1, blocking collectives, body(): tiles = lax.all_gather(rows, 'det', axis=0)  6.52 us
    all_to_all x1, waiting for transfers between devices, body(): heard = lax.all_to_all(sent, 'tm', split_axis=0, concat_axis=0, tiled=True)  5.85 us
    unnamed x26, local copies, waits for them, and re-layouts  5.72 us
    all_to_all x1, waiting for transfers between devices, body(): recv = lax.all_to_all(packed, 'tm', split_axis=0, concat_axis=0, tiled=True)  4.95 us
    ppermute x1, waiting for transfers between devices, body(): others.append(lax.ppermute(sent_on, 'det', ring))  3.59 us
  transfers between devices with their start and end apart: 4, of which 4 were waited for; matrix products, arithmetic and copies ran while one was open for 3% of the time, Pallas kernels for 4%

profile of v4, /device:TPU:0, one launch (start us, length us, event | category | flops | bytes accessed | tf_op | source)
XLA Modules:
  0.0 64.7 jit_solution(7104957288196513782)
XLA Ops:
  0.0 2.3 %shard_map.102 = (bf16[8,208,128]{2,1,0:T(8,128)(2,1)}, bf16[16,128]{1,0:T(8,128)(2,1)S(1)}) custom-call(s32[32]{0:T(128)} %bitcast.274, s32[32]{0:T(128)} %th_ref.1, s32[8,16]{1,0:T(8,128)} %slot_ref.1, s32[8,2048]{1,0:T(8,128)} %r_ref.1, s32[8,2048]{1,0:T(8,128)} %c_ref.1, bf16[8,2048]{1,0:T(8,128)(2,1)} %fr_ref.1, bf16[8,2048]{1,0:T(8,128)(2,1)} %fc_ref.1, ...), custom_call_target="tpu_custom_call" | custom-call | tf_op jit(solution)/shard_map/pallas_call | solution.py:583
  2.3 7.3 %all-to-all-start.4 = ((bf16[8,208,128]{2,1,0:T(8,128)(2,1)}), bf16[8,208,128]{2,1,0:T(8,128)(2,1)S(1)}, u32[]{:S(2)}, u32[]{:S(2)}) async-start(bf16[8,208,128]{2,1,0:T(8,128)(2,1)} %get-tuple-element.154), calls=%async_computation.4 | async-start | bytes 851968 | tf_op jit(solution)/shard_map/all_to_all | solution.py:602
  9.6 0.9 %pad_maximum_fusion.2 = bf16[400,128]{1,0:T(8,128)(2,1)S(1)} fusion(bf16[16,128]{1,0:T(8,128)(2,1)S(1)} %get-tuple-element.155, bf16[384,128]{1,0:T(8,128)(2,1)} %bitcast.273), kind=kLoop, calls=%fused_computation.162 | loop fusion | flops 204800 | bytes 204800 | tf_op jit(solution)/shard_map/concatenate | solution.py:603
  10.5 6.5 %all-gather = bf16[1600,128]{1,0:T(8,128)(2,1)S(1)} all-gather(bf16[400,128]{1,0:T(8,128)(2,1)S(1)} %pad_maximum_fusion.2), channel_id=2, replica_groups=mesh['det'=4,'tm'=8] {'det'}, dimensions={0}, use_global_device_ids=true | all-gather | bytes 512000 | tf_op jit(solution)/shard_map/all_gather | solution.py:604
  17.0 5.0 %all-to-all-done.4.recv_ref = bf16[8,208,128]{2,1,0:T(8,128)(2,1)S(1)} async-done(((bf16[8,208,128]{2,1,0:T(8,128)(2,1)}), bf16[8,208,128]{2,1,0:T(8,128)(2,1)S(1)}, u32[]{:S(2)}, u32[]{:S(2)}) %all-to-all-start.4) | async-done | bytes 426016 | tf_op jit(solution)/shard_map/all_to_all | solution.py:602
  22.0 7.1 %shard_map.103 = (bf16[8,208,128]{2,1,0:T(8,128)(2,1)}, f32[10,192,128]{2,1,0:T(8,128)S(1)}, f32[192,8]{1,0:T(8,128)S(1)}, f32[16,128]{1,0:T(8,128)S(1)}) custom-call(bf16[8,208,128]{2,1,0:T(8,128)(2,1)S(1)} %all-to-all-done.4.recv_ref, bf16[4,400,128]{2,1,0:T(8,128)(2,1)S(1)} %bitcast.259), custom_call_target="tpu_custom_call" | custom-call | tf_op jit(solution)/shard_map/pallas_call | solution.py:623
  29.1 3.5 %all-to-all-start.5 = ((bf16[8,208,128]{2,1,0:T(8,128)(2,1)}), bf16[8,208,128]{2,1,0:T(8,128)(2,1)S(1)}, u32[]{:S(2)}, u32[]{:S(2)}) async-start(bf16[8,208,128]{2,1,0:T(8,128)(2,1)} %get-tuple-element.156), calls=%async_computation.5 | async-start | bytes 851968 | tf_op jit(solution)/shard_map/all_to_all | solution.py:638
  32.6 0.1 slice.79
  32.7 0.1 pad_maximum_fusion.3
  32.8 0.6 reverse.1
  33.4 0.1 slice.159
  33.5 0.1 concatenate.25
  33.6 0.1 broadcast_in_dim.168.line_ref
  33.6 2.9 %shard_map.104.mat_ref = bf16[8,2176,128]{2,1,0:T(8,128)(2,1)S(1)} custom-call(f32[8,1,2304]{2,1,0:T(1,128)S(1)} %broadcast_in_dim.168.line_ref), custom_call_target="tpu_custom_call" | custom-call | tf_op jit(solution)/shard_map/pallas_call | solution.py:617
  36.5 2.0 %copy-done = bf16[8,2176,128]{2,1,0:T(8,128)(2,1)} copy-done((bf16[8,2176,128]{2,1,0:T(8,128)(2,1)}, bf16[8,2176,128]{2,1,0:T(8,128)(2,1)S(1)}, u32[]{:S(2)}) %copy-start) | copy-done | bytes 4456472
  38.5 5.9 %all-to-all-done.5.recv_ref = bf16[8,208,128]{2,1,0:T(8,128)(2,1)S(1)} async-done(((bf16[8,208,128]{2,1,0:T(8,128)(2,1)}), bf16[8,208,128]{2,1,0:T(8,128)(2,1)S(1)}, u32[]{:S(2)}, u32[]{:S(2)}) %all-to-all-start.5) | async-done | bytes 426016 | tf_op jit(solution)/shard_map/all_to_all | solution.py:638
  44.4 2.3 %copy-done.1 = bf16[8,2176,128]{2,1,0:T(8,128)(2,1)S(1)} copy-done((bf16[8,2176,128]{2,1,0:T(8,128)(2,1)S(1)}, bf16[8,2176,128]{2,1,0:T(8,128)(2,1)}, u32[]{:S(2)}) %copy-start.1) | copy-done | bytes 4456472
  46.7 10.5 %shard_map.105 = (f32[2,4,96,128]{3,2,1,0:T(8,128)S(1)}, bf16[2,4,96,128]{3,2,1,0:T(8,128)(2,1)S(1)}, s32[1]{0:T(128)}) custom-call(s32[1]{0:T(128)} %bitcast.76.core_ref, bf16[8,208,128]{2,1,0:T(8,128)(2,1)S(1)} %all-to-all-done.5.recv_ref, bf16[8,2176,128]{2,1,0:T(8,128)(2,1)S(1)} %copy-done.1, f32[8,1025]{1,0:T(8,128)S(1)} %copy-done.2, ...), custom_call_target="tpu_custom_call" | custom-call | tf_op jit(solution)/shard_map/pallas_call | solution.py:645
  57.2 0.1 collective-permute-start.2
  57.3 1.4 %collective-permute-done.2 = bf16[2,4,96,128]{3,2,1,0:T(8,128)(2,1)S(1)} collective-permute-done((bf16[2,4,96,128]{3,2,1,0:T(8,128)(2,1)S(1)}, bf16[2,4,96,128]{3,2,1,0:T(8,128)(2,1)S(1)}, u32[]{:S(2)}, u32[]{:S(2)}) %collective-permute-start.2) | collective-permute-done | bytes 196640 | tf_op jit(solution)/shard_map/ppermute | solution.py:662
  58.7 0.7 %collective-permute-start.3 = (bf16[4,96,128]{2,1,0:T(8,128)(2,1)S(1)}, bf16[4,96,128]{2,1,0:T(8,128)(2,1)S(1)}, u32[]{:S(2)}, u32[]{:S(2)}) collective-permute-start(bf16[4,96,128]{2,1,0:T(8,128)(2,1)S(1)} %fusion.68), channel_id=1, source_target_pairs={{0,16},{8,24},{16,0},{24,8},{1,17},{9,25},{17,1},{25,9},{2,18},{10... | collective-permute-start | bytes 294920 | tf_op jit(solution)/shard_map/ppermute | solution.py:672
  60.0 3.6 %collective-permute-done.3 = bf16[4,96,128]{2,1,0:T(8,128)(2,1)S(1)} collective-permute-done((bf16[4,96,128]{2,1,0:T(8,128)(2,1)S(1)}, bf16[4,96,128]{2,1,0:T(8,128)(2,1)S(1)}, u32[]{:S(2)}, u32[]{:S(2)}) %collective-permute-start.3) | collective-permute-done | bytes 98336 | tf_op jit(solution)/shard_map/ppermute | solution.py:672
  63.7 0.3 conditional.1
  64.0 0.7 %copy-done.6 = f32[4,3,32,128]{3,2,1,0:T(8,128)} copy-done((f32[4,3,32,128]{3,2,1,0:T(8,128)}, f32[4,3,32,128]{3,2,1,0:T(8,128)S(1)}, u32[]{:S(2)}) %copy-start.6) | copy-done | bytes 196632
  (26 shorter events, 0.1 us)
Async XLA Ops:
  0.0 32.6 %copy-start.2 = (f32[8,1025]{1,0:T(8,128)S(1)}, f32[8,1025]{1,0:T(8,128)}, u32[]{:S(2)}) copy-start(f32[8,1025]{1,0:T(8,128)} %coef_ref.1) | copy-start | bytes 98404
  2.3 19.7 %all-to-all-start.4 = ((bf16[8,208,128]{2,1,0:T(8,128)(2,1)}), bf16[8,208,128]{2,1,0:T(8,128)(2,1)S(1)}, u32[]{:S(2)}, u32[]{:S(2)}) async-start(bf16[8,208,128]{2,1,0:T(8,128)(2,1)} %get-tuple-element.154), calls=%async_computation.4 | async-start | bytes 851968 | tf_op jit(solution)/shard_map/all_to_all | solution.py:602
  29.1 15.3 %all-to-all-start.5 = ((bf16[8,208,128]{2,1,0:T(8,128)(2,1)}), bf16[8,208,128]{2,1,0:T(8,128)(2,1)S(1)}, u32[]{:S(2)}, u32[]{:S(2)}) async-start(bf16[8,208,128]{2,1,0:T(8,128)(2,1)} %get-tuple-element.156), calls=%async_computation.5 | async-start | bytes 851968 | tf_op jit(solution)/shard_map/all_to_all | solution.py:638
  36.5 2.0 %copy-start = (bf16[8,2176,128]{2,1,0:T(8,128)(2,1)}, bf16[8,2176,128]{2,1,0:T(8,128)(2,1)S(1)}, u32[]{:S(2)}) copy-start(bf16[8,2176,128]{2,1,0:T(8,128)(2,1)S(1)} %shard_map.104.mat_ref) | copy-start | bytes 13369348
  44.4 2.3 %copy-start.1 = (bf16[8,2176,128]{2,1,0:T(8,128)(2,1)S(1)}, bf16[8,2176,128]{2,1,0:T(8,128)(2,1)}, u32[]{:S(2)}) copy-start(bf16[8,2176,128]{2,1,0:T(8,128)(2,1)} %copy-done) | copy-start | bytes 13369348
  46.7 17.0 %copy-start.3 = (s32[8,2048]{1,0:T(8,128)S(1)}, s32[8,2048]{1,0:T(8,128)}, u32[]{:S(2)}) copy-start(s32[8,2048]{1,0:T(8,128)} %r_ref.1) | copy-start | bytes 196612
  46.7 17.0 %copy-start.4 = (s32[8,2048]{1,0:T(8,128)S(1)}, s32[8,2048]{1,0:T(8,128)}, u32[]{:S(2)}) copy-start(s32[8,2048]{1,0:T(8,128)} %c_ref.1) | copy-start | bytes 196612
  46.7 17.0 %copy-start.5 = (f32[8,2048]{1,0:T(8,128)S(1)}, f32[8,2048]{1,0:T(8,128)}, u32[]{:S(2)}) copy-start(f32[8,2048]{1,0:T(8,128)} %ang_ref.1) | copy-start | bytes 196612
  46.7 17.0 %copy-start.7 = (bf16[8,2048]{1,0:T(8,128)(2,1)S(1)}, bf16[8,2048]{1,0:T(8,128)(2,1)}, u32[]{:S(2)}) copy-start(bf16[8,2048]{1,0:T(8,128)(2,1)} %fr_ref.1) | copy-start | bytes 98308
  46.7 17.0 %copy-start.8 = (bf16[8,2048]{1,0:T(8,128)(2,1)S(1)}, bf16[8,2048]{1,0:T(8,128)(2,1)}, u32[]{:S(2)}) copy-start(bf16[8,2048]{1,0:T(8,128)(2,1)} %fc_ref.1) | copy-start | bytes 98308
  46.7 17.0 %copy-start.9 = (s32[8,16]{1,0:T(8,128)S(1)}, s32[8,16]{1,0:T(8,128)}, u32[]{:S(2)}) copy-start(s32[8,16]{1,0:T(8,128)} %slot_ref.1) | copy-start | bytes 1540
  46.7 17.0 %copy-start.10 = (s32[1,1,32]{2,1,0:T(1,128)S(1)}, s32[1,1,32]{2,1,0:T(1,128)}, u32[]{:S(2)}) copy-start(s32[1,1,32]{2,1,0:T(1,128)} %param.20) | copy-start | bytes 388
  46.7 17.0 %copy-start.11 = (s32[32]{0:T(128)S(1)}, s32[32]{0:T(128)}, u32[]{:S(2)}) copy-start(s32[32]{0:T(128)} %th_ref.1) | copy-start | bytes 388
  57.2 1.5 %collective-permute-start.2 = (bf16[2,4,96,128]{3,2,1,0:T(8,128)(2,1)S(1)}, bf16[2,4,96,128]{3,2,1,0:T(8,128)(2,1)S(1)}, u32[]{:S(2)}, u32[]{:S(2)}) collective-permute-start(bf16[2,4,96,128]{3,2,1,0:T(8,128)(2,1)S(1)} %get-tuple-element.162), channel_id=1, source_target_pairs={{0,8},{8,0},{16,24},{24,16},{1,9},{9,1},{17,25},{25,17},{2,10},{10... | collective-permute-start | bytes 589832 | tf_op jit(solution)/shard_map/ppermute | solution.py:662
  58.7 4.9 %collective-permute-start.3 = (bf16[4,96,128]{2,1,0:T(8,128)(2,1)S(1)}, bf16[4,96,128]{2,1,0:T(8,128)(2,1)S(1)}, u32[]{:S(2)}, u32[]{:S(2)}) collective-permute-start(bf16[4,96,128]{2,1,0:T(8,128)(2,1)S(1)} %fusion.68), channel_id=1, source_target_pairs={{0,16},{8,24},{16,0},{24,8},{1,17},{9,25},{17,1},{25,9},{2,18},{10... | collective-permute-start | bytes 294920 | tf_op jit(solution)/shard_map/ppermute | solution.py:672
  64.0 0.7 %copy-start.6 = (f32[4,3,32,128]{3,2,1,0:T(8,128)}, f32[4,3,32,128]{3,2,1,0:T(8,128)S(1)}, u32[]{:S(2)}) copy-start(f32[4,3,32,128]{3,2,1,0:T(8,128)S(1)} %get-tuple-element.484) | copy-start | bytes 589828

commit v5 on v4

--- a/solution.py
+++ b/solution.py
@@ -266,10 +266,17 @@
     for d in range(groups_det):
         scratch_ref[4 + d : 5 + d, :] = tiles_ref[d, tile_rows:, :].astype(f32)[0:1]
     ids_ref[...] = dot_nt(order, facts)
-    sorted_fields = []
-    for f in range(6):
-        field = jnp.concatenate([recv_ref[s, f * cap : (f + 1) * cap, :] for s in range(owners)], axis=0)
-        sorted_fields.append(dot_nn(order, field))
+    sorted_fields = dot_nn(
+        order,
+        jnp.concatenate(
+            [
+                jnp.concatenate([recv_ref[s, f * cap : (f + 1) * cap, :] for s in range(owners)], axis=0)
+                for f in range(6)
+            ],
+            axis=1,
+        ),
+    )
+    sorted_fields = [sorted_fields[:, f * width : (f + 1) * width] for f in range(6)]
     twice = 2.0 * (sorted_fields[4] + sorted_fields[5])
     reach = side // 2 + META
     upper = jnp.where(sorted_fields[0] >= side // 2, 1.0, 0.0)
@@ -339,27 +346,35 @@
     lax.fori_loop(0, lines, one, 0)
 
 
-def filter_lines(blocks_dev, kept, recv_ref, mat_ref, coef_ref, filt_ref, line_ref):
+def lines_kernel(blocks_dev, kept, cap, tile_dev, edge, recv_ref, line_ref, over_ref):
     owners, rows, width = recv_ref.shape
-    lines, padded, _ = line_ref.shape
+    lines = line_ref.shape[0]
     count = owners * blocks_dev
-    edge = (padded - count) // 2
-    spans = padded - count + 1
+    most = totals = jnp.zeros((4, width), f32)
+    for s in range(owners):
+        counts = recv_ref[s, kept : kept + META, :].astype(f32)[4:8]
+        most, totals = jnp.maximum(most, counts), totals + counts
+    most = jnp.max(most)
+    fullest = jnp.max(totals) + tile_dev * (GROUP - 1)
+    over_ref[0] = jnp.logical_or(most > cap, fullest > kept).astype(jnp.int32)
     together = math.gcd(owners, 8)
     line_ref[...] = jnp.zeros_like(line_ref)
 
     def some(first, lines_now, line0):
-        at, values = [], []
+        at, det, values = [], [], []
         for o in range(together):
             notes = recv_ref[first + o, kept:, :].astype(f32)
             notes = [notes[q * 8 : q * 8 + 8] for q in range(notes.shape[0] // 8)]
             notes = jnp.concatenate(notes, axis=1)[:, :kept]
-            row = notes[2:3] * count + notes[3:4] * blocks_dev + notes[1:2]
+            row = notes[3:4] * blocks_dev + notes[1:2]
             at.append(jnp.where(notes[0:1] > 0.5, row, -1.0))
+            det.append(notes[2:3])
             values.append(recv_ref[first + o, 0:kept, :])
-        at = jnp.concatenate(at, axis=1).astype(jnp.int32) - line0 * count
-        place = ones_where(iota((lines_now * count, together * kept), 0) == at)
-        return dot_nn(place, jnp.concatenate(values, axis=0))
+        at = jnp.concatenate(at, axis=1).astype(jnp.int32)
+        det = jnp.concatenate(det, axis=1)
+        place = ones_where(iota((count, together * kept), 0) == at)
+        place = [place * ones_where(det == line0 + d) for d in range(lines_now)]
+        return dot_nn(jnp.concatenate(place, axis=0), jnp.concatenate(values, axis=0))
 
     if together == owners:
         found = some(0, lines, 0)
@@ -373,6 +388,13 @@
             return carry
 
         lax.fori_loop(0, owners // together, one, 0)
+
+
+def filter_lines(line_ref, mat_ref, coef_ref, filt_ref):
+    lines, padded, width = line_ref.shape
+    count = filt_ref.shape[1]
+    spans = padded - count + 1
+    edge = spans // 2
     for d in range(lines):
         spread = jnp.concatenate([line_ref[d, m : m + count, :].astype(bf16) for m in range(spans)], axis=1)
         weight = coef_ref[d : d + 1, 0:1] + 1.0
@@ -382,9 +404,8 @@
 
 def back_kernel(
     blocks_dev,
-    cap,
     core_ref,
-    recv_ref,
+    line_ref,
     mat_ref,
     coef_ref,
     fields_ref,
@@ -392,26 +413,16 @@
     seg_ref,
     mine_ref,
     theirs_ref,
-    over_ref,
     filt_ref,
-    line_ref,
     scaled_ref,
     acc_ref,
 ):
     width = fields_ref.shape[2]
     kept = fields_ref.shape[1]
-    filter_lines(blocks_dev, kept, recv_ref, mat_ref, coef_ref, filt_ref, line_ref)
+    filter_lines(line_ref, mat_ref, coef_ref, filt_ref)
     pairs, tile_dev, rows_dev, side = mine_ref.shape
     part = rows_dev // 3
     core = core_ref[0]
-    owners = recv_ref.shape[0]
-    most = totals = jnp.zeros((4, width), f32)
-    for s in range(owners):
-        counts = recv_ref[s, kept : kept + META, :].astype(f32)[4:8]
-        most, totals = jnp.maximum(most, counts), totals + counts
-    most = jnp.max(most)
-    fullest = jnp.max(totals) + tile_dev * (GROUP - 1)
-    over_ref[0] = jnp.logical_or(most > cap, fullest > kept).astype(jnp.int32)
     lines, count, _ = filt_ref.shape
     ids = ids_ref[...]
     at = ids[:, 2:3] * count + ids[:, 3:4] * blocks_dev + ids[:, 1:2]
@@ -642,21 +653,28 @@
     core = lax.rem(place, 2)
     half = lax.div(place, 2)
     pairs = groups_det // 2
-    mine, theirs, over = call(
-        functools.partial(back_kernel, blocks, cap),
+    heard, over = call(
+        functools.partial(lines_kernel, blocks, kept, cap, tile_dev, spans // 2),
+        (
+            jax.ShapeDtypeStruct((dets, count + spans - 1, width), f32),
+            jax.ShapeDtypeStruct((1,), jnp.int32),
+        ),
+        in_specs=[vmem],
+        out_specs=(vmem, smem),
+    )(heard)
+    mine, theirs = call(
+        functools.partial(back_kernel, blocks),
         (
             jax.ShapeDtypeStruct((pairs, tile_dev, 3 * part, side), f32),
             jax.ShapeDtypeStruct((pairs, tile_dev, 3 * part, side), bf16),
-            jax.ShapeDtypeStruct((1,), jnp.int32),
         ),
         [
             pltpu.VMEM((dets, count, width), f32),
-            pltpu.VMEM((dets, count + spans - 1, width), f32),
             pltpu.VMEM((3, kept, width), f32),
             pltpu.VMEM((tile_dev, 3 * side, side), f32),
         ],
         in_specs=[smem] + [vmem] * 6,
-        out_specs=(vmem, vmem, smem),
+        out_specs=(vmem, vmem),
     )(core[None].astype(jnp.int32), heard, matrix, noise_coef, fields, ids, seg)
 
     beside = lax.ppermute(theirs, "det", [(i, i ^ 1) for i in range(groups_det)])

time: 65 us -> 62.6 us (0.963)
  Pallas kernels: 22.8 us -> 19.6 us
  starting transfers between devices: 11.5 us -> 12.6 us
    pallas_call x1 -> x2, Pallas kernels: 10.5 us -> 8.14 us  [the longest x1 6.63 us: body(): call(functools.partial(back_kernel, blocks), (jax.ShapeDtypeStruct((pairs...]
    ppermute x1, waiting for transfers between devices: 3.59 us -> 2.65 us  [body(): others.append(lax.ppermute(sent_on, 'det', ring))]
    ppermute x1, starting transfers between devices: 0.67 us -> 1.6 us  [body(): others.append(lax.ppermute(sent_on, 'det', ring))]
    pallas_call x1, Pallas kernels: 7.12 us -> 6.29 us  [body(): call(functools.partial(project_kernel, cap, kept, tile_dev), (jax.ShapeDt...]
  transfers between devices with their start and end apart: 4 -> 4, of which waited for: 4 -> 4; matrix products, arithmetic and copies ran while one was open for 3% -> 3% of each run, Pallas kernels for 4% -> 5%
where the time goes in v5:
time: 62.6 us; the launch traced here: 62.2 us
  Pallas kernels  19.6 us (31%)
  waiting for transfers between devices  15.4 us (25%)
  starting transfers between devices  12.6 us (20%)
  blocking collectives  6.52 us (10%)
  local copies, waits for them, and re-layouts  5.92 us (9%)
  other arithmetic  1.04 us (2%)
  between operations  0.86 us (1%)
    all_to_all x1, starting transfers between devices, body(): recv = lax.all_to_all(packed, 'tm', split_axis=0, concat_axis=0, tiled=True)  7.29 us
    pallas_call x1, Pallas kernels, body(): call(functools.partial(back_kernel, blocks), (jax.ShapeDtypeStruct((pairs...  6.63 us
    all_gather x1, blocking collectives, body(): tiles = lax.all_gather(rows, 'det', axis=0)  6.52 us
    all_to_all x1, waiting for transfers between devices, body(): heard = lax.all_to_all(sent, 'tm', split_axis=0, concat_axis=0, tiled=True)  6.42 us
    pallas_call x1, Pallas kernels, body(): call(functools.partial(project_kernel, cap, kept, tile_dev), (jax.ShapeDt...  6.29 us
    unnamed x26, local copies, waits for them, and re-layouts  5.71 us
    all_to_all x1, waiting for transfers between devices, body(): recv = lax.all_to_all(packed, 'tm', split_axis=0, concat_axis=0, tiled=True)  4.95 us
    all_to_all x1, starting transfers between devices, body(): heard = lax.all_to_all(sent, 'tm', split_axis=0, concat_axis=0, tiled=True)  3.63 us
  transfers between devices with their start and end apart: 4, of which 4 were waited for; matrix products, arithmetic and copies ran while one was open for 3% of the time, Pallas kernels for 5%

profile of v5, /device:TPU:0, one launch (start us, length us, event | category | flops | bytes accessed | tf_op | source)
XLA Modules:
  0.0 62.2 jit_solution(12456068770752363833)
XLA Ops:
  0.0 2.3 %shard_map.102 = (bf16[8,208,128]{2,1,0:T(8,128)(2,1)}, bf16[16,128]{1,0:T(8,128)(2,1)S(1)}) custom-call(s32[32]{0:T(128)} %bitcast.274, s32[32]{0:T(128)} %th_ref.1, s32[8,16]{1,0:T(8,128)} %slot_ref.1, s32[8,2048]{1,0:T(8,128)} %r_ref.1, s32[8,2048]{1,0:T(8,128)} %c_ref.1, bf16[8,2048]{1,0:T(8,128)(2,1)} %fr_ref.1, bf16[8,2048]{1,0:T(8,128)(2,1)} %fc_ref.1, ...), custom_call_target="tpu_custom_call" | custom-call | tf_op jit(solution)/shard_map/pallas_call | solution.py:594
  2.3 7.3 %all-to-all-start.4 = ((bf16[8,208,128]{2,1,0:T(8,128)(2,1)}), bf16[8,208,128]{2,1,0:T(8,128)(2,1)S(1)}, u32[]{:S(2)}, u32[]{:S(2)}) async-start(bf16[8,208,128]{2,1,0:T(8,128)(2,1)} %get-tuple-element.155), calls=%async_computation.4 | async-start | bytes 851968 | tf_op jit(solution)/shard_map/all_to_all | solution.py:613
  9.6 0.9 %pad_maximum_fusion.2 = bf16[400,128]{1,0:T(8,128)(2,1)S(1)} fusion(bf16[16,128]{1,0:T(8,128)(2,1)S(1)} %get-tuple-element.156, bf16[384,128]{1,0:T(8,128)(2,1)} %bitcast.273), kind=kLoop, calls=%fused_computation.162 | loop fusion | flops 204800 | bytes 204800 | tf_op jit(solution)/shard_map/concatenate | solution.py:614
  10.5 6.5 %all-gather = bf16[1600,128]{1,0:T(8,128)(2,1)S(1)} all-gather(bf16[400,128]{1,0:T(8,128)(2,1)S(1)} %pad_maximum_fusion.2), channel_id=2, replica_groups=mesh['det'=4,'tm'=8] {'det'}, dimensions={0}, use_global_device_ids=true | all-gather | bytes 512000 | tf_op jit(solution)/shard_map/all_gather | solution.py:615
  17.0 5.0 %all-to-all-done.4.recv_ref = bf16[8,208,128]{2,1,0:T(8,128)(2,1)S(1)} async-done(((bf16[8,208,128]{2,1,0:T(8,128)(2,1)}), bf16[8,208,128]{2,1,0:T(8,128)(2,1)S(1)}, u32[]{:S(2)}, u32[]{:S(2)}) %all-to-all-start.4) | async-done | bytes 426016 | tf_op jit(solution)/shard_map/all_to_all | solution.py:613
  22.0 6.3 %shard_map.103 = (bf16[8,208,128]{2,1,0:T(8,128)(2,1)}, f32[10,192,128]{2,1,0:T(8,128)S(1)}, f32[192,8]{1,0:T(8,128)S(1)}, f32[16,128]{1,0:T(8,128)S(1)}) custom-call(bf16[8,208,128]{2,1,0:T(8,128)(2,1)S(1)} %all-to-all-done.4.recv_ref, bf16[4,400,128]{2,1,0:T(8,128)(2,1)S(1)} %bitcast.259), custom_call_target="tpu_custom_call" | custom-call | tf_op jit(solution)/shard_map/pallas_call | solution.py:634
  28.3 3.6 %all-to-all-start.5 = ((bf16[8,208,128]{2,1,0:T(8,128)(2,1)}), bf16[8,208,128]{2,1,0:T(8,128)(2,1)S(1)}, u32[]{:S(2)}, u32[]{:S(2)}) async-start(bf16[8,208,128]{2,1,0:T(8,128)(2,1)} %get-tuple-element.157), calls=%async_computation.5 | async-start | bytes 851968 | tf_op jit(solution)/shard_map/all_to_all | solution.py:649
  31.9 0.1 slice.79
  32.0 0.1 pad_maximum_fusion.3
  32.1 0.6 %reverse.1 = f32[8,1152]{1,0:T(8,128)S(1)} reverse(f32[8,1152]{1,0:T(8,128)S(1)} %bitcast.272), dimensions={1} | reverse | bytes 73728
  32.7 0.1 slice.159
  32.8 0.1 concatenate.25
  33.0 2.9 %shard_map.105.mat_ref = bf16[8,2176,128]{2,1,0:T(8,128)(2,1)S(1)} custom-call(f32[8,1,2304]{2,1,0:T(1,128)S(1)} %broadcast_in_dim.168.line_ref), custom_call_target="tpu_custom_call" | custom-call | tf_op jit(solution)/shard_map/pallas_call | solution.py:628
  35.8 2.0 %copy-done = bf16[8,2176,128]{2,1,0:T(8,128)(2,1)} copy-done((bf16[8,2176,128]{2,1,0:T(8,128)(2,1)}, bf16[8,2176,128]{2,1,0:T(8,128)(2,1)S(1)}, u32[]{:S(2)}) %copy-start) | copy-done | bytes 4456472
  37.9 6.4 %all-to-all-done.5.recv_ref = bf16[8,208,128]{2,1,0:T(8,128)(2,1)S(1)} async-done(((bf16[8,208,128]{2,1,0:T(8,128)(2,1)}), bf16[8,208,128]{2,1,0:T(8,128)(2,1)S(1)}, u32[]{:S(2)}, u32[]{:S(2)}) %all-to-all-start.5) | async-done | bytes 426016 | tf_op jit(solution)/shard_map/all_to_all | solution.py:649
  44.3 1.5 %shard_map.104 = (f32[8,144,128]{2,1,0:T(8,128)S(1)}, s32[1]{0:T(128)}) custom-call(bf16[8,208,128]{2,1,0:T(8,128)(2,1)S(1)} %all-to-all-done.5.recv_ref), custom_call_target="tpu_custom_call" | custom-call | tf_op jit(solution)/shard_map/pallas_call | solution.py:656
  45.8 2.3 %copy-done.1 = bf16[8,2176,128]{2,1,0:T(8,128)(2,1)S(1)} copy-done((bf16[8,2176,128]{2,1,0:T(8,128)(2,1)S(1)}, bf16[8,2176,128]{2,1,0:T(8,128)(2,1)}, u32[]{:S(2)}) %copy-start.1) | copy-done | bytes 4456472
  48.1 6.6 %shard_map.106 = (f32[2,4,96,128]{3,2,1,0:T(8,128)S(1)}, bf16[2,4,96,128]{3,2,1,0:T(8,128)(2,1)S(1)}) custom-call(s32[1]{0:T(128)} %bitcast.80.core_ref, f32[8,144,128]{2,1,0:T(8,128)S(1)} %get-tuple-element.159.line_ref, bf16[8,2176,128]{2,1,0:T(8,128)(2,1)S(1)} %copy-done.1, f32[8,1025]{1,0:T(8,128)S(1)} %copy-done.2, ...), custom_call_target="tpu_custom_call" | custom-call | tf_op jit(solution)/shard_map/pallas_call | solution.py:665
  54.8 0.1 collective-permute-start.2
  54.9 1.4 %collective-permute-done.2 = bf16[2,4,96,128]{3,2,1,0:T(8,128)(2,1)S(1)} collective-permute-done((bf16[2,4,96,128]{3,2,1,0:T(8,128)(2,1)S(1)}, bf16[2,4,96,128]{3,2,1,0:T(8,128)(2,1)S(1)}, u32[]{:S(2)}, u32[]{:S(2)}) %collective-permute-start.2) | collective-permute-done | bytes 196640 | tf_op jit(solution)/shard_map/ppermute | solution.py:680
  56.3 1.6 %collective-permute-start.3 = (bf16[4,96,128]{2,1,0:T(8,128)(2,1)S(1)}, bf16[4,96,128]{2,1,0:T(8,128)(2,1)S(1)}, u32[]{:S(2)}, u32[]{:S(2)}) collective-permute-start(bf16[4,96,128]{2,1,0:T(8,128)(2,1)S(1)} %fusion.68), channel_id=1, source_target_pairs={{0,16},{8,24},{16,0},{24,8},{1,17},{9,25},{17,1},{25,9},{2,18},{10... | collective-permute-start | bytes 294920 | tf_op jit(solution)/shard_map/ppermute | solution.py:690
  58.5 2.6 %collective-permute-done.3 = bf16[4,96,128]{2,1,0:T(8,128)(2,1)S(1)} collective-permute-done((bf16[4,96,128]{2,1,0:T(8,128)(2,1)S(1)}, bf16[4,96,128]{2,1,0:T(8,128)(2,1)S(1)}, u32[]{:S(2)}, u32[]{:S(2)}) %collective-permute-start.3) | collective-permute-done | bytes 98336 | tf_op jit(solution)/shard_map/ppermute | solution.py:690
  61.3 0.3 conditional.1
  61.6 0.7 %copy-done.6 = f32[4,3,32,128]{3,2,1,0:T(8,128)} copy-done((f32[4,3,32,128]{3,2,1,0:T(8,128)}, f32[4,3,32,128]{3,2,1,0:T(8,128)S(1)}, u32[]{:S(2)}) %copy-start.6) | copy-done | bytes 196632
  (27 shorter events, 0.2 us)
Async XLA Ops:
  0.0 31.9 %copy-start.2 = (f32[8,1025]{1,0:T(8,128)S(1)}, f32[8,1025]{1,0:T(8,128)}, u32[]{:S(2)}) copy-start(f32[8,1025]{1,0:T(8,128)} %coef_ref.1) | copy-start | bytes 98404
  2.3 19.7 %all-to-all-start.4 = ((bf16[8,208,128]{2,1,0:T(8,128)(2,1)}), bf16[8,208,128]{2,1,0:T(8,128)(2,1)S(1)}, u32[]{:S(2)}, u32[]{:S(2)}) async-start(bf16[8,208,128]{2,1,0:T(8,128)(2,1)} %get-tuple-element.155), calls=%async_computation.4 | async-start | bytes 851968 | tf_op jit(solution)/shard_map/all_to_all | solution.py:613
  28.3 16.0 %all-to-all-start.5 = ((bf16[8,208,128]{2,1,0:T(8,128)(2,1)}), bf16[8,208,128]{2,1,0:T(8,128)(2,1)S(1)}, u32[]{:S(2)}, u32[]{:S(2)}) async-start(bf16[8,208,128]{2,1,0:T(8,128)(2,1)} %get-tuple-element.157), calls=%async_computation.5 | async-start | bytes 851968 | tf_op jit(solution)/shard_map/all_to_all | solution.py:649
  35.8 2.0 %copy-start = (bf16[8,2176,128]{2,1,0:T(8,128)(2,1)}, bf16[8,2176,128]{2,1,0:T(8,128)(2,1)S(1)}, u32[]{:S(2)}) copy-start(bf16[8,2176,128]{2,1,0:T(8,128)(2,1)S(1)} %shard_map.105.mat_ref) | copy-start | bytes 13369348
  45.8 2.3 %copy-start.1 = (bf16[8,2176,128]{2,1,0:T(8,128)(2,1)S(1)}, bf16[8,2176,128]{2,1,0:T(8,128)(2,1)}, u32[]{:S(2)}) copy-start(bf16[8,2176,128]{2,1,0:T(8,128)(2,1)} %copy-done) | copy-start | bytes 13369348
  48.1 13.1 %copy-start.3 = (s32[8,2048]{1,0:T(8,128)S(1)}, s32[8,2048]{1,0:T(8,128)}, u32[]{:S(2)}) copy-start(s32[8,2048]{1,0:T(8,128)} %r_ref.1) | copy-start | bytes 196612
  48.1 13.1 %copy-start.4 = (s32[8,2048]{1,0:T(8,128)S(1)}, s32[8,2048]{1,0:T(8,128)}, u32[]{:S(2)}) copy-start(s32[8,2048]{1,0:T(8,128)} %c_ref.1) | copy-start | bytes 196612
  48.1 13.1 %copy-start.5 = (f32[8,2048]{1,0:T(8,128)S(1)}, f32[8,2048]{1,0:T(8,128)}, u32[]{:S(2)}) copy-start(f32[8,2048]{1,0:T(8,128)} %ang_ref.1) | copy-start | bytes 196612
  48.1 13.1 %copy-start.7 = (bf16[8,2048]{1,0:T(8,128)(2,1)S(1)}, bf16[8,2048]{1,0:T(8,128)(2,1)}, u32[]{:S(2)}) copy-start(bf16[8,2048]{1,0:T(8,128)(2,1)} %fr_ref.1) | copy-start | bytes 98308
  48.1 13.2 %copy-start.8 = (bf16[8,2048]{1,0:T(8,128)(2,1)S(1)}, bf16[8,2048]{1,0:T(8,128)(2,1)}, u32[]{:S(2)}) copy-start(bf16[8,2048]{1,0:T(8,128)(2,1)} %fc_ref.1) | copy-start | bytes 98308
  48.1 13.1 %copy-start.9 = (s32[8,16]{1,0:T(8,128)S(1)}, s32[8,16]{1,0:T(8,128)}, u32[]{:S(2)}) copy-start(s32[8,16]{1,0:T(8,128)} %slot_ref.1) | copy-start | bytes 1540
  48.1 13.1 %copy-start.10 = (s32[1,1,32]{2,1,0:T(1,128)S(1)}, s32[1,1,32]{2,1,0:T(1,128)}, u32[]{:S(2)}) copy-start(s32[1,1,32]{2,1,0:T(1,128)} %param.20) | copy-start | bytes 388
  48.1 13.1 %copy-start.11 = (s32[32]{0:T(128)S(1)}, s32[32]{0:T(128)}, u32[]{:S(2)}) copy-start(s32[32]{0:T(128)} %th_ref.1) | copy-start | bytes 388
  54.8 1.5 %collective-permute-start.2 = (bf16[2,4,96,128]{3,2,1,0:T(8,128)(2,1)S(1)}, bf16[2,4,96,128]{3,2,1,0:T(8,128)(2,1)S(1)}, u32[]{:S(2)}, u32[]{:S(2)}) collective-permute-start(bf16[2,4,96,128]{3,2,1,0:T(8,128)(2,1)S(1)} %get-tuple-element.164), channel_id=1, source_target_pairs={{0,8},{8,0},{16,24},{24,16},{1,9},{9,1},{17,25},{25,17},{2,10},{10... | collective-permute-start | bytes 589832 | tf_op jit(solution)/shard_map/ppermute | solution.py:680
  56.3 4.9 %collective-permute-start.3 = (bf16[4,96,128]{2,1,0:T(8,128)(2,1)S(1)}, bf16[4,96,128]{2,1,0:T(8,128)(2,1)S(1)}, u32[]{:S(2)}, u32[]{:S(2)}) collective-permute-start(bf16[4,96,128]{2,1,0:T(8,128)(2,1)S(1)} %fusion.68), channel_id=1, source_target_pairs={{0,16},{8,24},{16,0},{24,8},{1,17},{9,25},{17,1},{25,9},{2,18},{10... | collective-permute-start | bytes 294920 | tf_op jit(solution)/shard_map/ppermute | solution.py:690
  61.5 0.7 %copy-start.6 = (f32[4,3,32,128]{3,2,1,0:T(8,128)}, f32[4,3,32,128]{3,2,1,0:T(8,128)S(1)}, u32[]{:S(2)}) copy-start(f32[4,3,32,128]{3,2,1,0:T(8,128)S(1)} %get-tuple-element.486) | copy-start | bytes 589828

commit v6 on v5

--- a/solution.py
+++ b/solution.py
@@ -172,10 +172,10 @@
     angle_low = (angle - angle_high.astype(f32)).astype(bf16)
     fields = [by_run(ref).astype(bf16) for ref in (r_ref, c_ref, fr_ref, fc_ref)]
     fields += [angle_high, angle_low]
-    for f, field in enumerate(fields):
-        sent = dot_nn(place, field).astype(bf16)
+    sent = dot_nn(place, jnp.concatenate(fields, axis=1)).astype(bf16)
+    for f in range(len(fields)):
         for o in range(owners):
-            out_ref[o, f * cap : (f + 1) * cap, :] = sent[o * cap : (o + 1) * cap]
+            out_ref[o, f * cap : (f + 1) * cap, :] = sent[o * cap : (o + 1) * cap, f * width : (f + 1) * width]
     sub = iota((8, runs), 0)
     lane_run = iota((8, runs), 1)
     facts = jnp.where(sub == 0, tile_row + 1, jnp.where(sub == 1, lane_run // dets, lane_run % dets))

time: 62.6 us -> 62.6 us (level)
    ppermute x1, starting transfers between devices: 1.6 us -> 0.71 us  [body(): others.append(lax.ppermute(sent_on, 'det', ring))]
    ppermute x1, waiting for transfers between devices: 2.65 us -> 3.54 us  [body(): others.append(lax.ppermute(sent_on, 'det', ring))]
    all_to_all x1, starting transfers between devices: 3.63 us -> 4.43 us  [body(): heard = lax.all_to_all(sent, 'tm', split_axis=0, concat_axis=0, tiled=True)]
    all_to_all x1, waiting for transfers between devices: 6.42 us -> 5.64 us  [body(): heard = lax.all_to_all(sent, 'tm', split_axis=0, concat_axis=0, tiled=True)]
where the time goes in v6:
time: 62.6 us; the launch traced here: 62.2 us
  Pallas kernels  19.6 us (31%)
  waiting for transfers between devices  15.5 us (25%)
  starting transfers between devices  12.5 us (20%)
  blocking collectives  6.53 us (10%)
  local copies, waits for them, and re-layouts  5.92 us (9%)
  other arithmetic  1.04 us (2%)
  between operations  0.86 us (1%)
    all_to_all x1, starting transfers between devices, body(): recv = lax.all_to_all(packed, 'tm', split_axis=0, concat_axis=0, tiled=True)  7.28 us
    pallas_call x1, Pallas kernels, body(): call(functools.partial(back_kernel, blocks), (jax.ShapeDtypeStruct((pairs...  6.64 us
    all_gather x1, blocking collectives, body(): tiles = lax.all_gather(rows, 'det', axis=0)  6.53 us
    pallas_call x1, Pallas kernels, body(): call(functools.partial(project_kernel, cap, kept, tile_dev), (jax.ShapeDt...  6.27 us
    unnamed x26, local copies, waits for them, and re-layouts  5.71 us
    all_to_all x1, waiting for transfers between devices, body(): heard = lax.all_to_all(sent, 'tm', split_axis=0, concat_axis=0, tiled=True)  5.64 us
    all_to_all x1, waiting for transfers between devices, body(): recv = lax.all_to_all(packed, 'tm', split_axis=0, concat_axis=0, tiled=True)  4.95 us
    all_to_all x1, starting transfers between devices, body(): heard = lax.all_to_all(sent, 'tm', split_axis=0, concat_axis=0, tiled=True)  4.43 us
  transfers between devices with their start and end apart: 4, of which 4 were waited for; matrix products, arithmetic and copies ran while one was open for 3% of the time, Pallas kernels for 5%

profile of v6, /device:TPU:0, one launch (start us, length us, event | category | flops | bytes accessed | tf_op | source)
XLA Modules:
  0.0 62.2 jit_solution(17696705930612696891)
XLA Ops:
  0.0 2.3 %shard_map.102 = (bf16[8,208,128]{2,1,0:T(8,128)(2,1)}, bf16[16,128]{1,0:T(8,128)(2,1)S(1)}) custom-call(s32[32]{0:T(128)} %bitcast.274, s32[32]{0:T(128)} %th_ref.1, s32[8,16]{1,0:T(8,128)} %slot_ref.1, s32[8,2048]{1,0:T(8,128)} %r_ref.1, s32[8,2048]{1,0:T(8,128)} %c_ref.1, bf16[8,2048]{1,0:T(8,128)(2,1)} %fr_ref.1, bf16[8,2048]{1,0:T(8,128)(2,1)} %fc_ref.1, ...), custom_call_target="tpu_custom_call" | custom-call | tf_op jit(solution)/shard_map/pallas_call | solution.py:594
  2.3 7.3 %all-to-all-start.4 = ((bf16[8,208,128]{2,1,0:T(8,128)(2,1)}), bf16[8,208,128]{2,1,0:T(8,128)(2,1)S(1)}, u32[]{:S(2)}, u32[]{:S(2)}) async-start(bf16[8,208,128]{2,1,0:T(8,128)(2,1)} %get-tuple-element.155), calls=%async_computation.4 | async-start | bytes 851968 | tf_op jit(solution)/shard_map/all_to_all | solution.py:613
  9.6 0.9 %pad_maximum_fusion.2 = bf16[400,128]{1,0:T(8,128)(2,1)S(1)} fusion(bf16[16,128]{1,0:T(8,128)(2,1)S(1)} %get-tuple-element.156, bf16[384,128]{1,0:T(8,128)(2,1)} %bitcast.273), kind=kLoop, calls=%fused_computation.162 | loop fusion | flops 204800 | bytes 204800 | tf_op jit(solution)/shard_map/concatenate | solution.py:614
  10.5 6.5 %all-gather = bf16[1600,128]{1,0:T(8,128)(2,1)S(1)} all-gather(bf16[400,128]{1,0:T(8,128)(2,1)S(1)} %pad_maximum_fusion.2), channel_id=2, replica_groups=mesh['det'=4,'tm'=8] {'det'}, dimensions={0}, use_global_device_ids=true | all-gather | bytes 512000 | tf_op jit(solution)/shard_map/all_gather | solution.py:615
  17.0 4.9 %all-to-all-done.4.recv_ref = bf16[8,208,128]{2,1,0:T(8,128)(2,1)S(1)} async-done(((bf16[8,208,128]{2,1,0:T(8,128)(2,1)}), bf16[8,208,128]{2,1,0:T(8,128)(2,1)S(1)}, u32[]{:S(2)}, u32[]{:S(2)}) %all-to-all-start.4) | async-done | bytes 426016 | tf_op jit(solution)/shard_map/all_to_all | solution.py:613
  22.0 6.3 %shard_map.103 = (bf16[8,208,128]{2,1,0:T(8,128)(2,1)}, f32[10,192,128]{2,1,0:T(8,128)S(1)}, f32[192,8]{1,0:T(8,128)S(1)}, f32[16,128]{1,0:T(8,128)S(1)}) custom-call(bf16[8,208,128]{2,1,0:T(8,128)(2,1)S(1)} %all-to-all-done.4.recv_ref, bf16[4,400,128]{2,1,0:T(8,128)(2,1)S(1)} %bitcast.259), custom_call_target="tpu_custom_call" | custom-call | tf_op jit(solution)/shard_map/pallas_call | solution.py:634
  28.2 4.4 %all-to-all-start.5 = ((bf16[8,208,128]{2,1,0:T(8,128)(2,1)}), bf16[8,208,128]{2,1,0:T(8,128)(2,1)S(1)}, u32[]{:S(2)}, u32[]{:S(2)}) async-start(bf16[8,208,128]{2,1,0:T(8,128)(2,1)} %get-tuple-element.157), calls=%async_computation.5 | async-start | bytes 851968 | tf_op jit(solution)/shard_map/all_to_all | solution.py:649
  32.7 0.1 slice.79
  32.8 0.1 pad_maximum_fusion.3
  32.8 0.6 %reverse.1 = f32[8,1152]{1,0:T(8,128)S(1)} reverse(f32[8,1152]{1,0:T(8,128)S(1)} %bitcast.272), dimensions={1} | reverse | bytes 73728
  33.5 0.1 slice.159
  33.6 0.1 concatenate.25
  33.7 2.9 %shard_map.105.mat_ref = bf16[8,2176,128]{2,1,0:T(8,128)(2,1)S(1)} custom-call(f32[8,1,2304]{2,1,0:T(1,128)S(1)} %broadcast_in_dim.168.line_ref), custom_call_target="tpu_custom_call" | custom-call | tf_op jit(solution)/shard_map/pallas_call | solution.py:628
  36.6 2.0 %copy-done = bf16[8,2176,128]{2,1,0:T(8,128)(2,1)} copy-done((bf16[8,2176,128]{2,1,0:T(8,128)(2,1)}, bf16[8,2176,128]{2,1,0:T(8,128)(2,1)S(1)}, u32[]{:S(2)}) %copy-start) | copy-done | bytes 4456472
  38.6 5.6 %all-to-all-done.5.recv_ref = bf16[8,208,128]{2,1,0:T(8,128)(2,1)S(1)} async-done(((bf16[8,208,128]{2,1,0:T(8,128)(2,1)}), bf16[8,208,128]{2,1,0:T(8,128)(2,1)S(1)}, u32[]{:S(2)}, u32[]{:S(2)}) %all-to-all-start.5) | async-done | bytes 426016 | tf_op jit(solution)/shard_map/all_to_all | solution.py:649
  44.3 1.5 %shard_map.104 = (f32[8,144,128]{2,1,0:T(8,128)S(1)}, s32[1]{0:T(128)}) custom-call(bf16[8,208,128]{2,1,0:T(8,128)(2,1)S(1)} %all-to-all-done.5.recv_ref), custom_call_target="tpu_custom_call" | custom-call | tf_op jit(solution)/shard_map/pallas_call | solution.py:656
  45.8 2.3 %copy-done.1 = bf16[8,2176,128]{2,1,0:T(8,128)(2,1)S(1)} copy-done((bf16[8,2176,128]{2,1,0:T(8,128)(2,1)S(1)}, bf16[8,2176,128]{2,1,0:T(8,128)(2,1)}, u32[]{:S(2)}) %copy-start.1) | copy-done | bytes 4456472
  48.1 6.6 %shard_map.106 = (f32[2,4,96,128]{3,2,1,0:T(8,128)S(1)}, bf16[2,4,96,128]{3,2,1,0:T(8,128)(2,1)S(1)}) custom-call(s32[1]{0:T(128)} %bitcast.80.core_ref, f32[8,144,128]{2,1,0:T(8,128)S(1)} %get-tuple-element.159.line_ref, bf16[8,2176,128]{2,1,0:T(8,128)(2,1)S(1)} %copy-done.1, f32[8,1025]{1,0:T(8,128)S(1)} %copy-done.2, ...), custom_call_target="tpu_custom_call" | custom-call | tf_op jit(solution)/shard_map/pallas_call | solution.py:665
  54.7 0.1 collective-permute-start.2
  54.8 1.4 %collective-permute-done.2 = bf16[2,4,96,128]{3,2,1,0:T(8,128)(2,1)S(1)} collective-permute-done((bf16[2,4,96,128]{3,2,1,0:T(8,128)(2,1)S(1)}, bf16[2,4,96,128]{3,2,1,0:T(8,128)(2,1)S(1)}, u32[]{:S(2)}, u32[]{:S(2)}) %collective-permute-start.2) | collective-permute-done | bytes 196640 | tf_op jit(solution)/shard_map/ppermute | solution.py:680
  56.3 0.7 %collective-permute-start.3 = (bf16[4,96,128]{2,1,0:T(8,128)(2,1)S(1)}, bf16[4,96,128]{2,1,0:T(8,128)(2,1)S(1)}, u32[]{:S(2)}, u32[]{:S(2)}) collective-permute-start(bf16[4,96,128]{2,1,0:T(8,128)(2,1)S(1)} %fusion.68), channel_id=1, source_target_pairs={{0,16},{8,24},{16,0},{24,8},{1,17},{9,25},{17,1},{25,9},{2,18},{10... | collective-permute-start | bytes 294920 | tf_op jit(solution)/shard_map/ppermute | solution.py:690
  57.6 3.5 %collective-permute-done.3 = bf16[4,96,128]{2,1,0:T(8,128)(2,1)S(1)} collective-permute-done((bf16[4,96,128]{2,1,0:T(8,128)(2,1)S(1)}, bf16[4,96,128]{2,1,0:T(8,128)(2,1)S(1)}, u32[]{:S(2)}, u32[]{:S(2)}) %collective-permute-start.3) | collective-permute-done | bytes 98336 | tf_op jit(solution)/shard_map/ppermute | solution.py:690
  61.2 0.3 conditional.1
  61.5 0.7 %copy-done.6 = f32[4,3,32,128]{3,2,1,0:T(8,128)} copy-done((f32[4,3,32,128]{3,2,1,0:T(8,128)}, f32[4,3,32,128]{3,2,1,0:T(8,128)S(1)}, u32[]{:S(2)}) %copy-start.6) | copy-done | bytes 196632
  (27 shorter events, 0.2 us)
Async XLA Ops:
  0.0 32.7 %copy-start.2 = (f32[8,1025]{1,0:T(8,128)S(1)}, f32[8,1025]{1,0:T(8,128)}, u32[]{:S(2)}) copy-start(f32[8,1025]{1,0:T(8,128)} %coef_ref.1) | copy-start | bytes 98404
  2.3 19.7 %all-to-all-start.4 = ((bf16[8,208,128]{2,1,0:T(8,128)(2,1)}), bf16[8,208,128]{2,1,0:T(8,128)(2,1)S(1)}, u32[]{:S(2)}, u32[]{:S(2)}) async-start(bf16[8,208,128]{2,1,0:T(8,128)(2,1)} %get-tuple-element.155), calls=%async_computation.4 | async-start | bytes 851968 | tf_op jit(solution)/shard_map/all_to_all | solution.py:613
  28.2 16.0 %all-to-all-start.5 = ((bf16[8,208,128]{2,1,0:T(8,128)(2,1)}), bf16[8,208,128]{2,1,0:T(8,128)(2,1)S(1)}, u32[]{:S(2)}, u32[]{:S(2)}) async-start(bf16[8,208,128]{2,1,0:T(8,128)(2,1)} %get-tuple-element.157), calls=%async_computation.5 | async-start | bytes 851968 | tf_op jit(solution)/shard_map/all_to_all | solution.py:649
  36.6 2.0 %copy-start = (bf16[8,2176,128]{2,1,0:T(8,128)(2,1)}, bf16[8,2176,128]{2,1,0:T(8,128)(2,1)S(1)}, u32[]{:S(2)}) copy-start(bf16[8,2176,128]{2,1,0:T(8,128)(2,1)S(1)} %shard_map.105.mat_ref) | copy-start | bytes 13369348
  45.8 2.3 %copy-start.1 = (bf16[8,2176,128]{2,1,0:T(8,128)(2,1)S(1)}, bf16[8,2176,128]{2,1,0:T(8,128)(2,1)}, u32[]{:S(2)}) copy-start(bf16[8,2176,128]{2,1,0:T(8,128)(2,1)} %copy-done) | copy-start | bytes 13369348
  48.0 13.1 %copy-start.3 = (s32[8,2048]{1,0:T(8,128)S(1)}, s32[8,2048]{1,0:T(8,128)}, u32[]{:S(2)}) copy-start(s32[8,2048]{1,0:T(8,128)} %r_ref.1) | copy-start | bytes 196612
  48.0 13.1 %copy-start.4 = (s32[8,2048]{1,0:T(8,128)S(1)}, s32[8,2048]{1,0:T(8,128)}, u32[]{:S(2)}) copy-start(s32[8,2048]{1,0:T(8,128)} %c_ref.1) | copy-start | bytes 196612
  48.0 13.1 %copy-start.5 = (f32[8,2048]{1,0:T(8,128)S(1)}, f32[8,2048]{1,0:T(8,128)}, u32[]{:S(2)}) copy-start(f32[8,2048]{1,0:T(8,128)} %ang_ref.1) | copy-start | bytes 196612
  48.0 13.1 %copy-start.7 = (bf16[8,2048]{1,0:T(8,128)(2,1)S(1)}, bf16[8,2048]{1,0:T(8,128)(2,1)}, u32[]{:S(2)}) copy-start(bf16[8,2048]{1,0:T(8,128)(2,1)} %fr_ref.1) | copy-start | bytes 98308
  48.0 13.2 %copy-start.8 = (bf16[8,2048]{1,0:T(8,128)(2,1)S(1)}, bf16[8,2048]{1,0:T(8,128)(2,1)}, u32[]{:S(2)}) copy-start(bf16[8,2048]{1,0:T(8,128)(2,1)} %fc_ref.1) | copy-start | bytes 98308
  48.1 13.2 %copy-start.9 = (s32[8,16]{1,0:T(8,128)S(1)}, s32[8,16]{1,0:T(8,128)}, u32[]{:S(2)}) copy-start(s32[8,16]{1,0:T(8,128)} %slot_ref.1) | copy-start | bytes 1540
  48.1 13.2 %copy-start.10 = (s32[1,1,32]{2,1,0:T(1,128)S(1)}, s32[1,1,32]{2,1,0:T(1,128)}, u32[]{:S(2)}) copy-start(s32[1,1,32]{2,1,0:T(1,128)} %param.20) | copy-start | bytes 388
  48.1 13.1 %copy-start.11 = (s32[32]{0:T(128)S(1)}, s32[32]{0:T(128)}, u32[]{:S(2)}) copy-start(s32[32]{0:T(128)} %th_ref.1) | copy-start | bytes 388
  54.7 1.5 %collective-permute-start.2 = (bf16[2,4,96,128]{3,2,1,0:T(8,128)(2,1)S(1)}, bf16[2,4,96,128]{3,2,1,0:T(8,128)(2,1)S(1)}, u32[]{:S(2)}, u32[]{:S(2)}) collective-permute-start(bf16[2,4,96,128]{3,2,1,0:T(8,128)(2,1)S(1)} %get-tuple-element.164), channel_id=1, source_target_pairs={{0,8},{8,0},{16,24},{24,16},{1,9},{9,1},{17,25},{25,17},{2,10},{10... | collective-permute-start | bytes 589832 | tf_op jit(solution)/shard_map/ppermute | solution.py:680
  56.3 4.9 %collective-permute-start.3 = (bf16[4,96,128]{2,1,0:T(8,128)(2,1)S(1)}, bf16[4,96,128]{2,1,0:T(8,128)(2,1)S(1)}, u32[]{:S(2)}, u32[]{:S(2)}) collective-permute-start(bf16[4,96,128]{2,1,0:T(8,128)(2,1)S(1)} %fusion.68), channel_id=1, source_target_pairs={{0,16},{8,24},{16,0},{24,8},{1,17},{9,25},{17,1},{25,9},{2,18},{10... | collective-permute-start | bytes 294920 | tf_op jit(solution)/shard_map/ppermute | solution.py:690
  61.5 0.7 %copy-start.6 = (f32[4,3,32,128]{3,2,1,0:T(8,128)}, f32[4,3,32,128]{3,2,1,0:T(8,128)S(1)}, u32[]{:S(2)}) copy-start(f32[4,3,32,128]{3,2,1,0:T(8,128)S(1)} %get-tuple-element.486) | copy-start | bytes 589828
